TPU v7x, 128 devices: a whole 4x4x4 slice. The times are simulated.
128 devices in a mesh: dp: 2 (over z_hi), seq: 16 (over z_lo, x, core), tp: 4 (over y).
Axes of the slice: x: 4, y: 4, z: 4 (z_hi: 2, z_lo: 2; z = z_hi * 2 + z_lo), core: 2. Of those that a mesh axis runs over, the one named last changes fastest.
Arguments:
- hidden_in: bfloat16 [6, 2048, 2048], P('dp', 'seq'), may hold values from -6 to 6
- segments: int32 [6, 2048], P('dp', 'seq'), may hold values from 0 to 3, as said below
- keep_mask: int32 [6, 2048], P('dp', 'seq'), may hold values 0 or 1
- ln_gain: float32 [2048], replicated, may hold values from 0.5 to 1.5
- ln_shift: float32 [2048], replicated, may hold values from -3 to 3
- w_qkv: float32 [2048, 3, 2048], P(('dp', 'seq'), None, 'tp'), may hold values from -0.125 to 0.125
- b_qkv: float32 [3, 2048], P(None, 'tp'), may hold values from -3 to 3
- w_dense: float32 [2048, 2048], P('tp', ('dp', 'seq')), may hold values from -0.5 to 0.5
- b_dense: float32 [2048], replicated, may hold values from -3 to 3
- w_up: float32 [2048, 8192], P(('dp', 'seq'), 'tp'), may hold values from -0.125 to 0.125
- b_up: float32 [8192], P('tp'), may hold values from -3 to 3
- w_down: float32 [8192, 2048], P('tp', ('dp', 'seq')), may hold values from -0.0625 to 0.0625
- b_down: float32 [2048], replicated, may hold values from -3 to 3
- cotangent: bfloat16 [6, 2048, 2048], P('dp', 'seq'), may hold values from -6 to 6
Outputs:
- block_out: float32 [6, 2048, 2048], P('dp', 'seq')
- input_grad: float32 [6, 2048, 2048], P('dp', 'seq')
- grad_gain: float32 [2048], replicated
- grad_shift: float32 [2048], replicated
- grad_qkv: float32 [2048, 3, 2048], P(('dp', 'seq'), None, 'tp')
- grad_bqkv: float32 [3, 2048], P(None, 'tp')
- grad_dense: float32 [2048, 2048], P('tp', ('dp', 'seq'))
- grad_bdense: float32 [2048], replicated
- grad_up: float32 [2048, 8192], P(('dp', 'seq'), 'tp')
- grad_bup: float32 [8192], P('tp')
- grad_down: float32 [8192, 2048], P('tp', ('dp', 'seq'))
- grad_bdown: float32 [2048], replicated
Inputs may be any that keep to these rules, and one draw needn't show every extreme that they name: `segments`: within each sequence the numbers start at 0 and never fall; in each group of 6 / 2 consecutive sequences one sequence, drawn from the seed, is a single document, and every other sequence holds four documents.
All inputs are finite; a program needn't handle non-finite values. No bound on the sum of `keep_mask` on one device may be relied on, other than what follows from the above.
Results may differ from a plain program's by a relative error of at most 0.02.
Values may be sent and summed in bfloat16 or wider, within the bound.
A program may use at most 320 MiB of HBM per device.

v0:
```python
import functools

import jax
import jax.numpy as jnp
from jax import lax
from jax.experimental import pallas as pl
from jax.experimental.pallas import tpu as pltpu
from jax.sharding import PartitionSpec as P

MESH = pl.DeviceIdType.MESH
HD = 64
ROT = 32
WINDOW = 1024
BF = jnp.bfloat16
F32 = jnp.float32
ANY = pl.BlockSpec(memory_space=pl.ANY)
VMEM = pl.BlockSpec(memory_space=pltpu.VMEM)


def wrap(v):
    return lax.rem(v + 4, 4)


def place():
    dp, sq, tp = lax.axis_index("dp"), lax.axis_index("seq"), lax.axis_index("tp")
    return dp * 2 + sq // 8, lax.rem(sq // 2, 4), lax.rem(sq, 2), tp


def device(z, x, c, y):
    z, x, y = wrap(z), wrap(x), wrap(y)
    return {"dp": z // 2, "seq": lax.rem(z, 2) * 8 + x * 2 + c, "tp": y}


class Net:
    def __init__(self, send, recv):
        self.send, self.recv, self.n, self.out, self.keys = send, recv, 0, {}, {}
        self.z, self.x, self.c, self.y = place()
        self.flip = 1 - 2 * lax.rem(self.z, 2)
        self.chip = lax.rem(self.z, 2) * 4 + self.x

    def to(self, axis, way):
        z, x, c, y = self.z, self.x, self.c, self.y
        if axis == "s":
            return device(z, x, 1 - c, y)
        if axis == "x":
            return device(z, x + way, c, y)
        if axis == "z":
            return device(z + way, x, c, y)
        if axis == "y":
            return device(z, x, c, y + way)
        return device(z + axis * self.flip, x + way, c, y)

    def greet(self, targets):
        bar = pltpu.get_barrier_semaphore()
        for axis, way in targets:
            pl.semaphore_signal(bar, inc=1, device_id=self.to(axis, way), device_id_type=MESH)
        pl.semaphore_wait(bar, len(targets))

    def chip_at(self, dz, dx):
        return lax.rem(lax.rem(self.z, 2) + dz, 2) * 4 + wrap(self.x + dx)

    def push(self, key, src, dst, axis, way):
        k = self.n
        self.n += 1
        copy = pltpu.make_async_remote_copy(
            src_ref=src,
            dst_ref=dst,
            send_sem=self.send.at[k],
            recv_sem=self.recv.at[k],
            device_id=self.to(axis, way),
            device_id_type=MESH,
        )
        copy.start()
        self.out[key] = copy
        self.keys[key] = copy

    def arrived(self, key):
        self.keys.pop(key).wait_recv()

    def sent(self, key):
        self.out.pop(key).wait_send()

    def drain(self):
        for key in list(self.out):
            self.sent(key)
        for key in list(self.keys):
            self.arrived(key)


def lanes(chip):
    return pl.ds(pl.multiple_of(chip * 128, 128), 128)


def dot(a, b, dims):
    return lax.dot_general(a, b, (dims, ((), ())), preferred_element_type=F32)


def span(start, size, unit=128):
    return pl.ds(pl.multiple_of(start, unit), size)


RING_XZ = (("x", 1), ("x", -1), ("z", 1), ("z", -1), ("s", 1))
RING_Y = (("y", 1), ("y", -1))
FAR = (("x", 2), ("z", 2), ("y", 2))
FARTHER = ((1, 1), (1, 2), (1, 3))
OTHERS = tuple((dz, dx) for dz in (1, 0) for dx in (2, 1, 3, 0) if dz or dx)
PARTS = 6
TILES = 4
LOW, HIGH, ALL = pl.ds(0, 512), pl.ds(512, 512), pl.ds(0, 1024)


class Gather:
    def __init__(self, net, name, src, dst):
        self.net, self.name, self.src, self.dst = net, name, src, dst
        self.half, self.quarter = src.shape[0] // 2, src.shape[0] // 4

    def at(self, h, a, b, r0, rn):
        n = self.net
        z, x = (n.z + b, n.x + a) if h == 0 else (n.z + a, n.x + b)
        return self.dst.at[wrap(z), wrap(x), n.c, pl.ds(h * self.half + r0, rn)]

    def own(self, h):
        return self.src.at[pl.ds(h * self.half, self.half)]

    def axes(self, h):
        return ("x", "z") if h == 0 else ("z", "x")

    def begin(self, sem):
        n = self.net
        for h in (0, 1):
            for w in (1, -1):
                n.push((self.name, h, "A", w), self.own(h), self.at(h, 0, 0, 0, self.half), self.axes(h)[0], w)
        for h in (0, 1):
            for w in (1, -1):
                n.push((self.name, h, "B", 0, w), self.own(h), self.at(h, 0, 0, 0, self.half), self.axes(h)[1], w)
        whole = self.dst.at[n.z, n.x, n.c]
        n.push((self.name, "s"), self.src, whole, "s", 1)
        self.local = pltpu.make_async_copy(self.src, whole, sem)
        self.local.start()

    def spread(self, h, a):
        n = self.net
        block = self.at(h, a, 0, 0, self.half)
        for w in (1, -1):
            n.push((self.name, h, "B", a, w), block, block, self.axes(h)[1], w)
        n.push((self.name, h, "s", a, 0), block, block, "s", 1)

    def near(self):
        n = self.net
        for h in (0, 1):
            for w in (1, -1):
                n.arrived((self.name, h, "A", w))
                part = self.at(h, -w, 0, 0 if w == 1 else self.quarter, self.quarter)
                n.push((self.name, h, "AF", w), part, part, self.axes(h)[0], w)
                self.spread(h, -w)

    def far(self):
        for h in (0, 1):
            for w in (1, -1):
                self.net.arrived((self.name, h, "AF", w))
            self.spread(h, 2)

    def pass_on(self, a):
        n = self.net
        for h in (0, 1):
            for w in (1, -1):
                n.arrived((self.name, h, "B", a, w))
                part = self.at(h, a, -w, 0 if w == 1 else self.quarter, self.quarter)
                n.push((self.name, h, "BF", a, w), part, part, self.axes(h)[1], w)
                block = self.at(h, a, -w, 0, self.half)
                n.push((self.name, h, "s", a, -w), block, block, "s", 1)

    def close(self, a):
        n = self.net
        for h in (0, 1):
            for w in (1, -1):
                n.arrived((self.name, h, "BF", a, w))
            block = self.at(h, a, 2, 0, self.half)
            n.push((self.name, h, "s", a, 2), block, block, "s", 1)


    def landed(self):
        n = self.net
        self.local.wait()
        n.arrived((self.name, "s"))
        for h in (0, 1):
            for a in (-1, 1, 2):
                n.arrived((self.name, h, "s", a, 0))
            for a in (0, -1, 1, 2):
                for b in (-1, 1, 2):
                    n.arrived((self.name, h, "s", a, b))


def turn(tensor, tables, sign):
    cosine, low, high = tables
    moved = pltpu.roll(tensor, 16, 1) * high[...] - pltpu.roll(tensor, 112, 1) * low[...]
    return tensor * cosine[...] + sign * moved


class Scatter:
    def __init__(self, net, name, acc, far1, near1, far2, near2, out):
        self.net, self.name, self.acc = net, name, acc
        self.far1, self.near1, self.far2, self.near2, self.out = far1, near1, far2, near2, out

    def axes(self, h):
        return ("z", "x") if h == 0 else ("x", "z")

    def first(self, h, d, r0, rn):
        n, rows = self.net, pl.ds(h * 32 + r0, rn)
        if h == 0:
            return self.acc.at[wrap(n.z + d), :, rows]
        return self.acc.at[:, wrap(n.x + d), rows]

    def second(self, h, d, r0, rn):
        n, rows = self.net, pl.ds(h * 32 + r0, rn)
        if h == 0:
            return self.acc.at[n.z, wrap(n.x + d), rows]
        return self.acc.at[wrap(n.z + d), n.x, rows]

    def step2(self):
        n = self.net
        for h in (0, 1):
            for k, w in ((0, -1), (1, 1)):
                n.push((self.name, h, "f1", w), self.first(h, 2, 16 * k, 16), self.far1.at[h, k], self.axes(h)[0], w)

    def step3(self):
        n = self.net
        for h in (0, 1):
            for k, w in ((0, -1), (1, 1)):
                n.arrived((self.name, h, "f1", w))
                part = self.first(h, w, 16 * k, 16)

                def add(t, carry):
                    part[t] = part[t] + self.far1[h, k, t]
                    return carry

                lax.fori_loop(0, 4, add, 0)
                n.push((self.name, h, "n1", w), self.first(h, w, 0, 32), self.near1.at[h, k], self.axes(h)[0], w)

    def step4(self):
        n = self.net
        for h in (0, 1):
            n.arrived((self.name, h, "n1", -1))
            n.arrived((self.name, h, "n1", 1))
            part = self.first(h, 0, 0, 32)

            def add(t, carry):
                for r in (0, 16):
                    rows = pl.ds(r, 16)
                    value = part[t, rows].astype(F32) + self.near1[h, 0, t, rows].astype(F32)
                    part[t, rows] = (value + self.near1[h, 1, t, rows].astype(F32)).astype(BF)
                return carry

            lax.fori_loop(0, 4, add, 0)
            for k, w in ((0, -1), (1, 1)):
                n.push((self.name, h, "f2", w), self.second(h, 2, 16 * k, 16), self.far2.at[h, k], self.axes(h)[1], w)

    def step5(self):
        n = self.net
        for h in (0, 1):
            for k, w in ((0, -1), (1, 1)):
                n.arrived((self.name, h, "f2", w))
                part = self.second(h, w, 16 * k, 16)
                part[...] = part[...] + self.far2[h, k]
                n.push((self.name, h, "n2", w), self.second(h, w, 0, 32), self.near2.at[h, k], self.axes(h)[1], w)

    def step6(self):
        n = self.net
        for h in (0, 1):
            n.arrived((self.name, h, "n2", -1))
            n.arrived((self.name, h, "n2", 1))
            part = self.second(h, 0, 0, 32)
            for r in (0, 16):
                rows = pl.ds(r, 16)
                value = part[rows].astype(F32) + self.near2[h, 0, rows].astype(F32)
                self.out[pl.ds(h * 32 + r, 16)] = value + self.near2[h, 1, rows].astype(F32)


class Sum:
    def __init__(self, net, name, acc, far, near, out):
        self.net, self.name, self.acc = net, name, acc
        self.far, self.near, self.out = far, near, out

    def block(self, d, r0, rn):
        start = pl.multiple_of(wrap(self.net.y + d) * 192 + r0, 16)
        return self.acc.at[pl.ds(start, rn)]

    def step1(self, value):
        n = self.net

        def fill(d, carry):
            for half in (0, 1):
                rows = pl.ds(pl.multiple_of(d * 192 + half * 96, 16), 96)
                held = value[pl.ds(pl.multiple_of(d * 96, 16), 96), pl.ds(half * 1024, 1024)]
                self.acc[rows] = held.astype(BF)
            return carry

        lax.fori_loop(0, 4, fill, 0)
        for k, w in ((0, -1), (1, 1)):
            n.push((self.name, "f", w), self.block(2, 96 * k, 96), self.far.at[k], "y", w)

    def step2(self):
        n = self.net
        for k, w in ((0, -1), (1, 1)):
            n.arrived((self.name, "f", w))
            part = self.block(w, 96 * k, 96)
            part[...] = part[...] + self.far[k]
            n.push((self.name, "n", w), self.block(w, 0, 192), self.near.at[k], "y", w)

    def step3(self, sem):
        n = self.net
        n.arrived((self.name, "n", -1))
        n.arrived((self.name, "n", 1))
        part = self.block(0, 0, 192)

        def add(t, carry):
            rows = pl.ds(pl.multiple_of(t * 16, 16), 16)
            value = part[rows].astype(F32) + self.near[0, rows].astype(F32)
            part[rows] = (value + self.near[1, rows].astype(F32)).astype(BF)
            return carry

        lax.fori_loop(0, 12, add, 0)
        for w in (-1, 1):
            n.push((self.name, "g", w), part, self.out.at[n.y], "y", w)
        self.last = pltpu.make_async_copy(part, self.out.at[n.y], sem)
        self.last.start()

    def step4(self):
        n = self.net
        for k, w in ((0, -1), (1, 1)):
            n.arrived((self.name, "g", w))
            part = self.out.at[wrap(n.y - w), pl.ds(96 * k, 96)]
            n.push((self.name, "gf", w), part, part, "y", w)

    def step5(self):
        self.last.wait()
        for w in (-1, 1):
            self.net.arrived((self.name, "gf", w))


def vector_sum(net, src, pairs, alongx, alongz, alongy, out):
    z, x, c, y = net.z, net.x, net.c, net.y
    pairs[c] = src[...]
    net.push("vs", pairs.at[c], pairs.at[c], "s", 1)
    yield
    net.arrived("vs")
    alongx[x] = pairs[0] + pairs[1]
    for w in (1, -1, 2):
        net.push(("vx", w), alongx.at[x], alongx.at[x], "x", w)
    yield
    for w in (1, -1, 2):
        net.arrived(("vx", w))
    alongz[z] = (alongx[0] + alongx[1]) + (alongx[2] + alongx[3])
    for w in (1, -1, 2):
        net.push(("vz", w), alongz.at[z], alongz.at[z], "z", w)
    yield
    for w in (1, -1, 2):
        net.arrived(("vz", w))
    alongy[y] = (alongz[0] + alongz[1]) + (alongz[2] + alongz[3])
    out[...] = alongy[y]
    for w in (1, -1, 2):
        net.push(("vy", w), alongy.at[y], alongy.at[y], "y", w)
    yield
    for w in (1, -1, 2):
        net.arrived(("vy", w))
    out[0:2] = (alongy[0, 0:2] + alongy[1, 0:2]) + (alongy[2, 0:2] + alongy[3, 0:2])
    yield


def halves(a, b, left):
    return jnp.where(left, a, pltpu.roll(b, 64, 1)), jnp.where(left, pltpu.roll(a, 64, 1), b)


def front_kernel(
    hidden, upstream, gain, shift, w_qkv, b_qkv, w_dense, w_up, b_up, w_down, info, t_cos, t_low, t_high, *refs
):
    gathered, refs = refs[:PARTS], refs[PARTS:]
    in_t, up_t, pairs, od_in, dkv_in, share, d_share, bias_up, refs = *refs[:8], refs[8:]
    shards, inputs, staged, kept, weights, qd, kv, qd_all, kv_all, info_all, seen, total, refs = *refs[:12], refs[12:]
    od, dkv, theirs, ours, pair, send, recv, loc = refs
    net = Net(send, recv)
    me, c = net.chip, net.c
    tables = (t_cos, t_low, t_high)
    lane = lax.broadcasted_iota(jnp.int32, (128, 128), 1)
    row = lax.broadcasted_iota(jnp.int32, (128, 128), 0)
    left = lane < 64
    mine = span(c * 384, 384)
    sems = iter(range(40))

    def here(src, dst):
        copy = pltpu.make_async_copy(src, dst, loc.at[next(sems)])
        copy.start()
        return copy

    for k in range(4):
        columns = pl.ds(k * 128, 128)
        pieces = halves(w_qkv[1, :, columns], w_qkv[2, :, columns], left[:64])
        for j in (0, 1):
            shards[0, :, pl.ds(256 * k + 128 * j, 128)] = pieces[j].astype(BF)
        shards[1, :, columns] = w_qkv[0, :, columns].astype(BF)
        shards[1, :, pl.ds(512 + 128 * k, 128)] = w_dense[:, columns].astype(BF)
    net.greet(RING_XZ + FARTHER + (("x", 2),))
    parts = [Gather(net, u, shards.at[u], gathered[u]) for u in range(PARTS)]
    parts[0].begin(loc.at[next(sems)])
    parts[1].begin(loc.at[next(sems)])
    for u in range(TILES):
        shards[2 + u, :, LOW] = w_up[:, pl.ds(u * 512, 512)].astype(BF)
        shards[2 + u, :, HIGH] = w_down[:, pl.ds(u * 512, 512)].astype(BF)

    def norm(t, carry):
        rows = span(t * 16, 16, 16)
        value = hidden[rows].astype(F32)
        value = value - jnp.mean(value, axis=1, keepdims=True)
        value = value * lax.rsqrt(jnp.mean(value * value, axis=1, keepdims=True) + 1e-05)
        inputs[rows] = (value * gain[...] + shift[...]).astype(BF)
        return carry

    lax.fori_loop(0, 24, norm, 0)

    def transpose(t, carry):
        columns, rows = span(t * 128, 128), span(t * 64, 64, 64)
        for k, src in enumerate((inputs, upstream)):
            tile = src[:, columns].T
            first, second = tile[:64], tile[64:]
            kept[k, rows] = jnp.where(c == 0, first, second)
            staged[k, rows] = jnp.where(c == 0, second, first)
        return carry

    lax.fori_loop(0, 16, transpose, 0)
    stays = []
    for k, dst in enumerate((in_t, up_t)):
        stays.append(here(kept.at[k], dst.at[c]))
        net.push(("t", k), staged.at[k], dst.at[c], "s", 1)

    def load(u):
        parts[u].landed()
        return here(gathered[u], weights.at[u % 4].reshape(4, 4, 2, 64, 1024))

    for u in (0, 1):
        parts[u].near()
    parts[2].begin(loc.at[next(sems)])
    for u in (0, 1):
        parts[u].far()
    for a in (0, -1, 1, 2):
        for u in (0, 1):
            parts[u].pass_on(a)
    for a in (0, -1, 1, 2):
        for u in (0, 1):
            parts[u].close(a)
    parts[2].near()
    parts[3].begin(loc.at[next(sems)])
    loads = {u: load(u) for u in (0, 1)}

    loads[0].wait()

    def keys_values(h, carry):
        columns = span(h * 256, 256)
        value = dot(inputs[...], weights[0, :, columns], ((1,), (0,)))
        bk, bv = b_qkv[1:2, span(h * 128, 128)], b_qkv[2:3, span(h * 128, 128)]
        bias = halves(bk, bv, left[:1])
        for j in (0, 1):
            tile = value[:, 128 * j : 128 * j + 128] + bias[j]
            for s in range(3):
                piece = tile[128 * s : 128 * s + 128]
                kv[s, :, span(h * 256 + 128 * j, 128)] = jnp.where(left, turn(piece, tables, 1.0), piece).astype(BF)
        return carry

    lax.fori_loop(0, 4, keys_values, 0)
    for dz, dx in OTHERS:
        other = net.chip_at(dz, dx)
        net.push(("k", dz, dx), kv.at[:, :, lanes(other)], kv_all.at[:, 2 * me + c], dz, dx)
        net.push(("i", dz, dx), info, info_all.at[2 * me + c], dz, dx)
    net.push("ks", kv.at[:, :, lanes(me)], kv_all.at[:, 2 * me + c], "s", 1)
    net.push("is", info, info_all.at[2 * me + c], "s", 1)
    stays.append(here(kv.at[:, :, lanes(me)], kv_all.at[:, 2 * me + c]))
    stays.append(here(info, info_all.at[2 * me + c]))
    loads[1].wait()

    def queries(h, carry):
        columns = span(h * 128, 128)
        q = dot(inputs[...], weights[1, :, columns], ((1,), (0,))) + b_qkv[0:1, columns]
        d = dot(upstream[...], weights[1, :, span(512 + h * 128, 128)], ((1,), (0,)))
        for s in range(3):
            pieces = halves(turn(q[128 * s : 128 * s + 128], tables, 1.0), d[128 * s : 128 * s + 128], left)
            for j in (0, 1):
                qd[s, :, span(h * 256 + 128 * j, 128)] = pieces[j].astype(BF)
        return carry

    lax.fori_loop(0, 4, queries, 0)
    for dz, dx in OTHERS:
        net.push(("q", dz, dx), qd.at[:, :, lanes(net.chip_at(dz, dx))], qd_all.at[me], dz, dx)
    stays.append(here(qd.at[:, :, lanes(me)], qd_all.at[me]))

    def units(u):
        slot = (2 + u) % 4
        loads[2 + u].wait()

        def some(j, carry):
            low, high = span(j * 256, 256), span(512 + j * 256, 256)
            unit = span(u * 512 + j * 256, 256)
            v = dot(inputs[...], weights[slot, :, low], ((1,), (0,))) + b_up[:, unit]
            d = dot(upstream[...], weights[slot, :, high], ((1,), (0,)))
            k = 0.7978845608028654
            square = v * v
            t = jnp.tanh(k * v * (1.0 + 0.044715 * square))
            half = 0.5 * (1.0 + t)
            slope = half + 0.5 * v * (1.0 - t * t) * (k * (1.0 + 0.134145 * square))
            d_up = (d * slope).astype(BF)
            pair[u, :, low] = d_up
            pair[u, :, high] = (v * half).astype(BF)
            bias_up[:, unit] = jnp.sum(d_up.astype(F32), axis=0, keepdims=True)
            return carry

        lax.fori_loop(0, 2, some, 0)
        net.push(("p", u), pair.at[u], pairs.at[u, mine], "s", 1)
        stays.append(here(pair.at[u], pairs.at[u, mine]))
        for total_ref, columns in ((d_share, LOW), (share, HIGH)):
            value = pair[u, :, columns]

            def spread(j, carry):
                rows = span(j * 512, 512)
                added = dot(value, weights[slot, rows, columns], ((1,), (1,)))
                if u == 0:
                    total_ref[:, rows] = added
                else:
                    total_ref[:, rows] += added
                return carry

            lax.fori_loop(0, 4, spread, 0)

    def attend(s, i, blocks, own, first):
        width = blocks * 128
        begin = first * 128 if isinstance(first, int) else pl.multiple_of(first * 128, 128)
        tile = qd_all[i, s].astype(F32)
        both_halves = [jnp.where(left, tile * (HD**-0.5), 0.0), jnp.where(left, 0.0, tile)]
        asking = jnp.concatenate(both_halves, axis=0).astype(BF)
        keys = kv_all[s, pl.ds(first, blocks)].reshape(width, 128)
        both = dot(asking, keys, ((1,), (1,)))
        asked = jnp.broadcast_to(info_all[own, pl.ds(3 + s, 1), :].astype(F32), (128, 128)).T
        held = seen[pl.ds(s, 1), pl.ds(begin, width)].astype(F32)
        pieces = []
        for b in range(blocks):
            fits = asked == held[:, b * 128 : (b + 1) * 128]
            if isinstance(first, int):
                if b >= blocks - 2:
                    ahead = lane + (b * 128 - own * 128) - row
                    fits = (fits | (ahead == 0)) & (ahead <= 0)
            elif b == blocks - 1:
                fits = (fits | (lane == row)) & (lane <= row)
            elif b == 0:
                fits = fits & (lane > row)
            pieces.append(jnp.where(fits, both[:128, b * 128 : (b + 1) * 128], -1e30))
        scores = jnp.concatenate(pieces, axis=1)
        expo = jnp.exp(scores - jnp.max(scores, axis=1, keepdims=True))
        probs = expo * (1.0 / jnp.sum(expo, axis=1, keepdims=True))
        d_probs = both[128:]
        delta = jnp.sum(probs * d_probs, axis=1, keepdims=True)
        mixed = jnp.concatenate([(probs * (d_probs - delta)).astype(BF), probs.astype(BF)], axis=0)
        back = dot(mixed, keys, ((1,), (0,)))
        od[i, s] = jnp.where(left, back[:128] * (HD**-0.5), back[128:]).astype(BF)
        total[pl.ds(begin, width)] += dot(mixed, asking, ((0,), (0,)))

    def sequence(s):
        total[...] = jnp.zeros_like(total)
        for i in range(4):
            attend(s, i, 2 * i + 2, 2 * i + c, 0)

        def late(i, carry):
            attend(s, i, 9, 2 * i + c, 2 * i + c - 8)
            return carry

        lax.fori_loop(4, 8, late, 0)
        dkv[s] = total[...].astype(BF).reshape(8, 2, 128, 128)

    parts[2].far()
    for a in (0, -1, 1, 2):
        parts[2].pass_on(a)
    parts[3].near()
    parts[4].begin(loc.at[next(sems)])
    for a in (0, -1, 1, 2):
        parts[2].close(a)
    for dz, dx in OTHERS:
        slot = 2 * net.chip_at(dz, -dx) + c
        net.arrived(("k", dz, dx))
        net.push(("ks", dz, dx), kv_all.at[:, slot], kv_all.at[:, slot], "s", 1)
        net.arrived(("i", dz, dx))
        net.push(("is", dz, dx), info_all.at[slot], info_all.at[slot], "s", 1)
    parts[3].far()
    loads[2] = load(2)
    for a in (0, -1, 1, 2):
        parts[3].pass_on(a)
    parts[4].near()
    parts[5].begin(loc.at[next(sems)])
    for dz, dx in OTHERS:
        for kind in ("q", "ks", "is"):
            net.arrived((kind, dz, dx))
    net.arrived("ks")
    net.arrived("is")
    for copy in stays:
        copy.wait()
    stays.clear()
    for b in range(16):
        seen[:, b * 128 : (b + 1) * 128] = info_all[b]
    sequence(0)
    for a in (0, -1, 1, 2):
        parts[3].close(a)
    parts[4].far()
    for a in (0, -1, 1):
        parts[4].pass_on(a)
    parts[5].near()
    parts[4].pass_on(2)
    sequence(1)
    parts[5].far()
    for a in (0, -1, 1, 2):
        parts[4].close(a)
    for a in (0, -1, 1):
        parts[5].pass_on(a)
    sequence(2)
    net.push("b", dkv.at[:, :, 1 - c], theirs, "s", 1)
    mixed = here(dkv.at[:, :, c], ours)
    stays.append(here(od.at[me], od_in.at[:, :, lanes(me)]))
    for dz, dx in OTHERS:
        net.push(("o", dz, dx), od.at[net.chip_at(dz, dx)], od_in.at[:, :, lanes(me)], dz, dx)
    mixed.wait()
    net.arrived("b")
    ours[...] = ours[...] + theirs[...]
    for dz, dx in OTHERS:
        net.push(("d", dz, dx), ours.at[:, net.chip_at(dz, dx)], dkv_in.at[:, :, lanes(me)], dz, dx)
    stays.append(here(ours.at[:, me], dkv_in.at[:, :, lanes(me)]))
    parts[5].pass_on(2)
    for a in (0, -1, 1, 2):
        parts[5].close(a)
    loads[3] = load(3)
    loads[4] = load(4)
    units(0)
    units(1)
    loads[5] = load(5)
    units(2)
    units(3)
    for copy in stays:
        copy.wait()
    net.drain()


def forward(args, cid):
    big = jax.ShapeDtypeStruct((4, 4, 2, 64, 1024), BF)
    factor = jax.ShapeDtypeStruct((2, 1024, 384), BF)
    heads = jax.ShapeDtypeStruct((3, 128, 1024), BF)
    wide = jax.ShapeDtypeStruct((384, 2048), F32)
    return pl.pallas_call(
        front_kernel,
        out_shape=[big] * PARTS
        + [factor, factor, jax.ShapeDtypeStruct((TILES, 768, 1024), BF), heads, heads]
        + [wide, wide, jax.ShapeDtypeStruct((1, 2048), F32)],
        in_specs=[VMEM] * len(args),
        out_specs=[ANY] * (PARTS + 5) + [VMEM] * 3,
        scratch_shapes=[
            pltpu.VMEM((PARTS, 64, 1024), BF),
            pltpu.VMEM((384, 2048), BF),
            pltpu.VMEM((2, 1024, 384), BF),
            pltpu.VMEM((2, 1024, 384), BF),
            pltpu.VMEM((4, 2048, 1024), BF),
            pltpu.VMEM((3, 128, 1024), BF),
            pltpu.VMEM((3, 128, 1024), BF),
            pltpu.VMEM((8, 3, 128, 128), BF),
            pltpu.VMEM((3, 16, 128, 128), BF),
            pltpu.VMEM((16, 8, 128), jnp.int32),
            pltpu.VMEM((8, 2048), jnp.int32),
            pltpu.VMEM((2048, 128), F32),
            pltpu.VMEM((8, 3, 128, 128), BF),
            pltpu.VMEM((3, 8, 2, 128, 128), BF),
            pltpu.VMEM((3, 8, 128, 128), BF),
            pltpu.VMEM((3, 8, 128, 128), BF),
            pltpu.VMEM((TILES, 384, 1024), BF),
            pltpu.SemaphoreType.DMA((540,)),
            pltpu.SemaphoreType.DMA((540,)),
            pltpu.SemaphoreType.DMA((40,)),
        ],
        compiler_params=pltpu.CompilerParams(
            collective_id=cid, has_side_effects=True, vmem_limit_bytes=62 * 2**20
        ),
        name="forward",
    )(*args)


def back_kernel(
    od_in, dkv_in, upstream, hidden, in_t, up_t, pairs, heads_w0, heads_w1, share_in, d_share_in, bias_up, gain, t_cos,
    t_low, t_high, input_grad, sum0, sum1, done, vec_out, *refs,
):
    accs, refs = refs[:PARTS], refs[PARTS:]
    far1, near1, far2, near2, refs = *refs[:4], refs[4:]
    weights, pair, factors, share, d_share, refs = *refs[:5], refs[5:]
    y_far, y_near, vecs, vec_acc, cores, alongx, alongz, alongy, send, recv, loc = refs
    net = Net(send, recv)
    c = net.c
    tables = (t_cos, t_low, t_high)
    left = lax.broadcasted_iota(jnp.int32, (128, 128), 1) < 64
    mine = span(c * 384, 384)
    sems = iter(range(40))

    def here(src, dst):
        copy = pltpu.make_async_copy(src, dst, loc.at[next(sems)])
        copy.start()
        return copy

    factor_loads = [here(src.at[k], factors.at[j, :, pl.ds(384 * k, 384)]) for j, src in enumerate((in_t, up_t)) for k in (0, 1)]
    pair_loads = {u: here(pairs.at[u], pair.at[u]) for u in (0, 1)}
    weight_loads = [here(src, weights.at[k]) for k, src in enumerate((heads_w0, heads_w1))]
    share_loads = [here(d_share_in, d_share), here(share_in, share)]
    net.greet(RING_XZ + RING_Y + FAR)
    parts = [
        Scatter(net, ("g", i), accs[i], far1.at[i], near1.at[i], far2.at[i], near2.at[i], done.at[i])
        for i in range(PARTS)
    ]

    def rows_of(s, carry):
        own = span(c * 384 + s * 128, 128)
        for h in range(8):
            columns = pl.ds(h * 128, 128)
            value = dkv_in[s, :, columns].astype(F32)
            pair[2, own, columns] = jnp.where(left, turn(value, tables, -1.0), value).astype(BF)
        for h in range(4):
            a = od_in[s, :, 256 * h : 256 * h + 128].astype(F32)
            b = od_in[s, :, 256 * h + 128 : 256 * h + 256].astype(F32)
            asked, got = halves(a, b, left)
            pair[3, own, pl.ds(h * 128, 128)] = turn(asked, tables, -1.0).astype(BF)
            pair[3, own, pl.ds(512 + h * 128, 128)] = got.astype(BF)
        return carry

    lax.fori_loop(0, 3, rows_of, 0)
    for slot in (2, 3):
        rows = pair.at[slot, mine]
        net.push(("p", slot), rows, rows, "s", 1)

    def gradients(u, slot, first_t, second_t):
        acc = accs[u]

        def some(z, carry):
            rows = span(z * 256, 256)
            for k, j in enumerate((first_t, second_t)):
                columns = pl.ds(k * 512, 512)
                value = dot(factors[j, rows], pair[slot, :, columns], ((1,), (0,)))
                acc[z, :, :, columns] = value.astype(BF).reshape(4, 64, 512)
            return carry

        lax.fori_loop(0, 4, some, 0)
        parts[u].step2()

    def tile(u):
        pair_loads[u].wait()
        gradients(u, u % 2, 0, 1)
        if u + 2 < TILES:
            pair_loads[u + 2] = here(pairs.at[u + 2], pair.at[u % 2])

    def spread(total, slot, columns):
        value = pair[slot, mine, columns]

        def chunk(j, carry):
            rows = span(j * 512, 512)
            total[:, rows] += dot(value, weights[slot - 2, rows, columns], ((1,), (1,)))
            return carry

        lax.fori_loop(0, 4, chunk, 0)

    def normed(rows):
        value = hidden[rows].astype(F32)
        value = value - jnp.mean(value, axis=1, keepdims=True)
        inverse = lax.rsqrt(jnp.mean(value * value, axis=1, keepdims=True) + 1e-05)
        return value * inverse, inverse

    def vectors():
        vec_acc[...] = jnp.zeros_like(vec_acc)
        vecs[...] = jnp.zeros_like(vecs)

        def chunk(t, carry):
            rows = span(t * 16, 16, 16)
            standard, _ = normed(rows)
            value = d_share[rows]
            for k, item in enumerate((value * standard, value, upstream[rows].astype(F32))):
                vec_acc[k] += item[:8] + item[8:]
            return carry

        lax.fori_loop(0, 24, chunk, 0)
        for k in range(3):
            vecs[k : k + 1] = jnp.sum(vec_acc[k], axis=0, keepdims=True)
        vecs[3:4] = bias_up[...]
        for k in range(4):
            columns = pl.ds(k * 256, 256)
            vecs[4:5, columns] = jnp.sum(pair[2, mine, columns].astype(F32), axis=0, keepdims=True)
        vecs[4:5, 1024:1536] = jnp.sum(pair[3, mine, LOW].astype(F32), axis=0, keepdims=True)

    def finish_in():
        def chunk(t, carry):
            rows = span(t * 16, 16, 16)
            base = t // 6 * 192 + lax.rem(t, 6) * 16
            standard, inverse = normed(rows)
            got = [weights[1, span(base + 96 * k, 16, 16)].astype(F32) for k in (0, 1)]
            scaled = jnp.concatenate(got, axis=1) * gain[...]
            mean = jnp.mean(scaled, axis=1, keepdims=True)
            along = jnp.mean(scaled * standard, axis=1, keepdims=True)
            d_share[rows] = upstream[rows].astype(F32) + inverse * (scaled - mean - standard * along)
            return carry

        lax.fori_loop(0, 24, chunk, 0)

    ys = [
        Sum(net, "yi", weights.at[0, pl.ds(0, 768)], y_far.at[0], y_near.at[0], sum0),
        Sum(net, "yo", weights.at[0, pl.ds(768, 768)], y_far.at[1], y_near.at[1], sum1),
    ]
    for copy in factor_loads:
        copy.wait()
    tile(0)
    tile(1)
    for copy in weight_loads + share_loads:
        copy.wait()
    spread(d_share, 2, ALL)
    spread(d_share, 3, LOW)
    ys[0].step1(d_share)
    spread(share, 3, HIGH)
    ys[1].step1(share)
    parts[0].step3()
    for slot in (2, 3):
        net.arrived(("p", slot))
    gradients(4, 2, 0, 0)
    ys[0].step2()
    parts[1].step3()
    gradients(5, 3, 0, 1)
    ys[1].step2()
    vectors()
    vec = vector_sum(net, vecs, cores, alongx, alongz, alongy, vec_out)
    next(vec)
    parts[0].step4()
    ys[0].step3(loc.at[next(sems)])
    tile(2)
    parts[4].step3()
    parts[1].step4()
    next(vec)
    ys[1].step3(loc.at[next(sems)])
    tile(3)
    parts[0].step5()
    parts[5].step3()
    ys[0].step4()
    parts[4].step4()
    next(vec)
    parts[1].step5()
    parts[0].step6()
    parts[2].step3()
    ys[1].step4()
    parts[5].step4()
    next(vec)
    parts[4].step5()
    parts[1].step6()
    parts[3].step3()
    ys[0].step5()
    got0 = here(sum0, weights.at[1, pl.ds(0, 768)].reshape(4, 192, 1024))
    parts[2].step4()
    next(vec)
    parts[5].step5()
    parts[4].step6()
    got0.wait()
    finish_in()
    out0 = here(d_share, input_grad)
    parts[3].step4()
    parts[2].step5()
    parts[5].step6()
    ys[1].step5()
    parts[3].step5()
    parts[2].step6()
    parts[3].step6()
    out0.wait()
    net.drain()


def backward(args, cid):
    wide = jax.ShapeDtypeStruct((384, 2048), F32)
    return pl.pallas_call(
        back_kernel,
        out_shape=[wide]
        + [jax.ShapeDtypeStruct((4, 192, 1024), BF)] * 2
        + [jax.ShapeDtypeStruct((PARTS, 64, 1024), F32), jax.ShapeDtypeStruct((8, 2048), F32)],
        in_specs=[VMEM] * 4 + [ANY] * 7 + [VMEM] * 5,
        out_specs=[ANY] * 3 + [VMEM] * 2,
        scratch_shapes=[pltpu.VMEM((4, 4, 64, 1024), BF)] * PARTS
        + [
            pltpu.VMEM((PARTS, 2, 2, 4, 16, 1024), BF),
            pltpu.VMEM((PARTS, 2, 2, 4, 32, 1024), BF),
            pltpu.VMEM((PARTS, 2, 2, 16, 1024), BF),
            pltpu.VMEM((PARTS, 2, 2, 32, 1024), BF),
            pltpu.VMEM((2, 2048, 1024), BF),
            pltpu.VMEM((4, 768, 1024), BF),
            pltpu.VMEM((2, 1024, 768), BF),
            pltpu.VMEM((384, 2048), F32),
            pltpu.VMEM((384, 2048), F32),
            pltpu.VMEM((2, 2, 96, 1024), BF),
            pltpu.VMEM((2, 2, 192, 1024), BF),
            pltpu.VMEM((8, 2048), F32),
            pltpu.VMEM((3, 8, 2048), F32),
            pltpu.VMEM((2, 8, 2048), F32),
            pltpu.VMEM((4, 8, 2048), F32),
            pltpu.VMEM((4, 8, 2048), F32),
            pltpu.VMEM((4, 8, 2048), F32),
            pltpu.SemaphoreType.DMA((140,)),
            pltpu.SemaphoreType.DMA((140,)),
            pltpu.SemaphoreType.DMA((40,)),
        ],
        compiler_params=pltpu.CompilerParams(
            collective_id=cid, has_side_effects=True, vmem_limit_bytes=63 * 2**20
        ),
        name="backward",
    )(*args)


def finish_kernel(
    hidden, summed, b_dense, b_down, grad, done, vecs, block_out, input_grad, g_qkv, g_dense, g_up, g_down, v_gain,
    v_shift, v_out, v_up, v_qkv, v_out2,
):
    for half in (0, 1):
        columns = pl.ds(half * 1024, 1024)
        bias = b_dense[:, columns] + b_down[:, columns]
        got = summed[0, pl.ds(96 * half, 96)].astype(F32)
        block_out[:, columns] = hidden[:, columns].astype(F32) + got + bias
    input_grad[...] = grad[...]

    @pl.when(pl.program_id(0) == 0)
    def _():
        left = lax.broadcasted_iota(jnp.int32, (64, 128), 1) < 64
        for u in range(TILES):
            g_up[:, pl.ds(u * 512, 512)] = done[u, :, :512]
            g_down[:, pl.ds(u * 512, 512)] = done[u, :, 512:]
        g_qkv[0] = done[5, :, :512]
        g_dense[...] = done[5, :, 512:]
        v_qkv[0:1] = vecs[4:5, 1024:1536]
        for k in range(4):
            a, b = pl.ds(256 * k, 128), pl.ds(256 * k + 128, 128)
            pieces = halves(done[4, :, a], done[4, :, b], left)
            rows = halves(vecs[4:5, a], vecs[4:5, b], left[:1])
            for j in (0, 1):
                g_qkv[1 + j, :, pl.ds(k * 128, 128)] = pieces[j]
                v_qkv[1 + j : 2 + j, pl.ds(k * 128, 128)] = rows[j]
        for k, dst in ((0, v_gain), (1, v_shift), (2, v_out), (2, v_out2), (3, v_up)):
            dst[...] = vecs[k]


def finish(hidden, summed, b_dense, b_down, grad, done, vecs):
    wide, row = jax.ShapeDtypeStruct((384, 2048), F32), jax.ShapeDtypeStruct((2048,), F32)
    rows = pl.BlockSpec((96, 2048), lambda i: (i, 0))
    small = [
        jax.ShapeDtypeStruct((3, 64, 512), F32),
        jax.ShapeDtypeStruct((64, 512), F32),
        jax.ShapeDtypeStruct((64, 2048), F32),
        jax.ShapeDtypeStruct((64, 2048), F32),
        row,
        row,
        row,
        row,
        jax.ShapeDtypeStruct((3, 512), F32),
        row,
    ]

    def whole(shape):
        return pl.BlockSpec(shape, lambda i: (0,) * len(shape))

    return pl.pallas_call(
        finish_kernel,
        grid=(4,),
        out_shape=[wide, wide] + small,
        in_specs=[rows, pl.BlockSpec((1, 192, 1024), lambda i: (i, 0, 0)), whole((1, 2048)), whole((1, 2048)), rows]
        + [whole((PARTS, 64, 1024)), whole((8, 2048))],
        out_specs=[rows, rows] + [whole(s.shape) for s in small],
        compiler_params=pltpu.CompilerParams(vmem_limit_bytes=62 * 2**20),
        name="finish",
    )(hidden, summed, b_dense, b_down, grad, done, vecs)


def local(
    hidden_in, segments, keep_mask, ln_gain, ln_shift, w_qkv, b_qkv, w_dense, b_dense, w_up, b_up, w_down, b_down,
    cotangent,
):
    rows, width = 384, 2048
    positions = lax.axis_index("seq") * 128 + jnp.arange(128, dtype=jnp.int32)
    half = ROT // 2
    frequency = 10000.0 ** (-(jnp.arange(half, dtype=F32) * 2.0) / ROT)
    quiet = jnp.zeros((HD - ROT,), F32)
    places = jnp.arange(128, dtype=jnp.int32) % HD
    turned = positions.astype(F32)[:, None] * jnp.concatenate([frequency, frequency, quiet] * 2)[None, :]
    t_cos = jnp.cos(turned)
    t_low = jnp.where(places < half, jnp.sin(turned), 0.0)
    t_high = jnp.where(places >= half, jnp.sin(turned), 0.0)
    tables = [t_cos, t_low, t_high]
    info = jnp.concatenate(
        [jnp.where(keep_mask > 0, segments, -1), segments, jnp.zeros((2, 128), jnp.int32)], axis=0
    )
    hidden = hidden_in.reshape(rows, width)
    upstream = cotangent.reshape(rows, width)
    outs = forward(
        [hidden, upstream, ln_gain[None], ln_shift[None], w_qkv.transpose(1, 0, 2), b_qkv, w_dense.T, w_up]
        + [b_up[None], w_down.T, info, *tables],
        0,
    )
    heads_w = [w.reshape(2048, 1024) for w in outs[:2]]
    in_t, up_t, pairs, od_in, dkv_in, share, d_share, bias_up = outs[PARTS:]
    input_grad, _, summed, done, vectors = backward(
        [od_in, dkv_in, upstream, hidden, in_t, up_t, pairs, *heads_w, share, d_share, bias_up, ln_gain[None], *tables], 1
    )
    block_out, input_grad, grad_qkv, grad_dense, grad_up, grad_down, gain, shift, out, up, grad_bqkv, out2 = finish(
        hidden, summed, b_dense[None], b_down[None], input_grad, done, vectors
    )
    return (
        block_out.reshape(3, 128, width),
        input_grad.reshape(3, 128, width),
        gain,
        shift,
        grad_qkv.transpose(1, 0, 2),
        grad_bqkv,
        grad_dense.T,
        out,
        grad_up,
        up,
        grad_down.T,
        out2,
    )


def solution(mesh):
    return jax.shard_map(
        local,
        mesh=mesh,
        in_specs=(
            P("dp", "seq", None),
            P("dp", "seq"),
            P("dp", "seq"),
            P(),
            P(),
            P(("dp", "seq"), None, "tp"),
            P(None, "tp"),
            P("tp", ("dp", "seq")),
            P(),
            P(("dp", "seq"), "tp"),
            P("tp"),
            P("tp", ("dp", "seq")),
            P(),
            P("dp", "seq", None),
        ),
        out_specs=(
            P("dp", "seq", None),
            P("dp", "seq", None),
            P(),
            P(),
            P(("dp", "seq"), None, "tp"),
            P(None, "tp"),
            P("tp", ("dp", "seq")),
            P(),
            P(("dp", "seq"), "tp"),
            P("tp"),
            P("tp", ("dp", "seq")),
            P(),
        ),
        check_vma=False,
    )
```

profile of v0, /device:TPU:0, one launch (start us, length us, event | category | flops | bytes accessed | tf_op | source)
XLA Modules:
  0.0 264.5 jit_solution(662950438244764855)
XLA Ops:
  0.7 0.1 pad.2.clone
  0.8 0.1 concatenate.7
  0.8 0.7 compare_select_fusion
  1.6 1.3 add_add_fusion.info
  2.9 1.0 fusion
  3.9 159.4 %forward.1 = (bf16[4,4,2,64,1024]{4,3,2,1,0:T(8,128)(2,1)}, bf16[4,4,2,64,1024]{4,3,2,1,0:T(8,128)(2,1)}, bf16[4,4,2,64,1024]{4,3,2,1,0:T(8,128)(2,1)}, bf16[4,4...) custom-call(bf16[384,2048]{1,0:T(8,128)(2,1)} %bitcast.17, ...), custom_call_target="tpu_custom_call" | custom-call | tf_op jit(solution)/shard_map/forward/pallas_call | solution.py:650
  163.3 93.7 %backward.1 = (f32[384,2048]{1,0:T(8,128)}, bf16[4,192,1024]{2,1,0:T(8,128)(2,1)}, bf16[4,192,1024]{2,1,0:T(8,128)(2,1)}, f32[6,64,1024]{2,1,0:T(8,128)}, f32[8,2048]{1,0:T(8,128)}) custom-call(bf16[3,128,1024]{2,1,0:T(8,128)(2,1)} %get-tuple-element.38.od_in, bf16[3,128,1024]{2,1,0:T(8,128)(2,1)} %get-tuple-element.39.dkv_in, bf16[384,2048]{1,0:T(8,128)(2,1)} %bitcast.21, ...), custom_call_target="tpu_custom_call" | custom-call | tf_op jit(solution)/shard_map/backward/pallas_call | solution.py:876
  257.0 7.3 %finish.1 = (f32[384,2048]{1,0:T(8,128)}, f32[384,2048]{1,0:T(8,128)}, f32[3,64,512]{2,1,0:T(8,128)}, f32[64,512]{1,0:T(8,128)}, f32[64,2048]{1,0:T(8,128)}, /*i...) custom-call(bf16[384,2048]{1,0:T(8,128)(2,1)} %bitcast.19, ...), custom_call_target="tpu_custom_call" | custom-call | tf_op jit(solution)/shard_map/finish/pallas_call | solution.py:963
  (5 shorter events, 0.0 us)
where the time goes:
time: 265 us; the launch traced here: 264 us
  Pallas kernels  260 us (98%)
  other arithmetic  3.06 us (1%)
    pallas_call x1, Pallas kernels, forward(): pl.pallas_call(front_kernel, out_shape=[big] * PARTS + [factor, factor, j...  159 us
    pallas_call x1, Pallas kernels, backward(): pl.pallas_call(back_kernel, out_shape=[wide] + [jax.ShapeDtypeStruct((4,...  93.7 us
    pallas_call x1, Pallas kernels, finish(): pl.pallas_call(finish_kernel, grid=(4,), out_shape=[wide, wide] + small,...  7.32 us

commit v1 on v0

--- a/solution.py
+++ b/solution.py
@@ -2,6 +2,7 @@
 
 import jax
 import jax.numpy as jnp
+import numpy as np
 from jax import lax
 from jax.experimental import pallas as pl
 from jax.experimental.pallas import tpu as pltpu
@@ -114,6 +115,78 @@
         self.net, self.name, self.src, self.dst = net, name, src, dst
         self.half, self.quarter = src.shape[0] // 2, src.shape[0] // 4
 
+    def axes(self, h):
+        return ("x", "z") if h == 0 else ("z", "x")
+
+    def block(self, h, a, r0, rn):
+        n, rows = self.net, pl.ds(h * self.half + r0, rn)
+        if h == 0:
+            return self.dst.at[n.z, wrap(n.x + a), n.c, rows]
+        return self.dst.at[wrap(n.z + a), n.x, n.c, rows]
+
+    def line(self, h, b, r0, rn):
+        n, rows = self.net, pl.ds(h * self.half + r0, rn)
+        if h == 0:
+            return self.dst.at[wrap(n.z + b), :, n.c, rows]
+        return self.dst.at[:, wrap(n.x + b), n.c, rows]
+
+    def begin(self, sem):
+        n = self.net
+        for h in (0, 1):
+            own = self.src.at[pl.ds(h * self.half, self.half)]
+            for w in (1, -1):
+                n.push((self.name, h, "A", w), own, self.block(h, 0, 0, self.half), self.axes(h)[0], w)
+        self.local = pltpu.make_async_copy(self.src, self.dst.at[n.z, n.x, n.c], sem)
+        self.local.start()
+
+    def near(self):
+        n = self.net
+        for h in (0, 1):
+            for w in (1, -1):
+                n.arrived((self.name, h, "A", w))
+                part = self.block(h, -w, 0 if w == 1 else self.quarter, self.quarter)
+                n.push((self.name, h, "AF", w), part, part, self.axes(h)[0], w)
+
+    def far(self):
+        n = self.net
+        self.local.wait()
+        for h in (0, 1):
+            for w in (1, -1):
+                n.arrived((self.name, h, "AF", w))
+            line = self.line(h, 0, 0, self.half)
+            for w in (1, -1):
+                n.push((self.name, h, "B", w), line, line, self.axes(h)[1], w)
+            n.push((self.name, h, "s", 0), line, line, "s", 1)
+
+    def pass_on(self):
+        n = self.net
+        for h in (0, 1):
+            for w in (1, -1):
+                n.arrived((self.name, h, "B", w))
+                part = self.line(h, -w, 0 if w == 1 else self.quarter, self.quarter)
+                n.push((self.name, h, "BF", w), part, part, self.axes(h)[1], w)
+                line = self.line(h, -w, 0, self.half)
+                n.push((self.name, h, "s", -w), line, line, "s", 1)
+
+    def close(self):
+        n = self.net
+        for h in (0, 1):
+            for w in (1, -1):
+                n.arrived((self.name, h, "BF", w))
+            line = self.line(h, 2, 0, self.half)
+            n.push((self.name, h, "s", 2), line, line, "s", 1)
+
+    def landed(self):
+        for h in (0, 1):
+            for b in (0, -1, 1, 2):
+                self.net.arrived((self.name, h, "s", b))
+
+
+class FineGather:
+    def __init__(self, net, name, src, dst):
+        self.net, self.name, self.src, self.dst = net, name, src, dst
+        self.half, self.quarter = src.shape[0] // 2, src.shape[0] // 4
+
     def at(self, h, a, b, r0, rn):
         n = self.net
         z, x = (n.z + b, n.x + a) if h == 0 else (n.z + a, n.x + b)
@@ -178,7 +251,6 @@
             block = self.at(h, a, 2, 0, self.half)
             n.push((self.name, h, "s", a, 2), block, block, "s", 1)
 
-
     def landed(self):
         n = self.net
         self.local.wait()
@@ -189,6 +261,16 @@
             for a in (0, -1, 1, 2):
                 for b in (-1, 1, 2):
                     n.arrived((self.name, h, "s", a, b))
+
+
+def fill_tables(tables, near_cos, near_sin, base_cos, base_sin):
+    own = pl.ds(lax.axis_index("seq"), 1)
+    cosine, sine = base_cos[own], base_sin[own]
+    place_in = lax.rem(lax.broadcasted_iota(jnp.int32, (128, 128), 1), HD)
+    tables[0][...] = near_cos[...] * cosine - near_sin[...] * sine
+    total = near_sin[...] * cosine + near_cos[...] * sine
+    tables[1][...] = jnp.where(place_in < ROT // 2, total, 0.0)
+    tables[2][...] = jnp.where(place_in < ROT // 2, 0.0, total)
 
 
 def turn(tensor, tables, sign):
@@ -372,12 +454,14 @@
 
 
 def front_kernel(
-    hidden, upstream, gain, shift, w_qkv, b_qkv, w_dense, w_up, b_up, w_down, info, t_cos, t_low, t_high, *refs
+    hidden_in, upstream_in, w_up_in, w_down_in, gain, shift, w_qkv, b_qkv, w_dense, b_up, segments, keep,
+    near_cos, near_sin, base_cos, base_sin, *refs,
 ):
     gathered, refs = refs[:PARTS], refs[PARTS:]
-    in_t, up_t, pairs, od_in, dkv_in, share, d_share, bias_up, refs = *refs[:8], refs[8:]
+    in_t, up_t, pairs, od_in, dkv_in, share_out, d_share_out, bias_up, refs = *refs[:8], refs[8:]
     shards, inputs, staged, kept, weights, qd, kv, qd_all, kv_all, info_all, seen, total, refs = *refs[:12], refs[12:]
-    od, dkv, theirs, ours, pair, send, recv, loc = refs
+    od, dkv, theirs, ours, pair, share, d_share, hidden, upstream, w_up, w_down, info, refs = *refs[:12], refs[12:]
+    t_cos, t_low, t_high, send, recv, loc = refs
     net = Net(send, recv)
     me, c = net.chip, net.c
     tables = (t_cos, t_low, t_high)
@@ -385,27 +469,30 @@
     row = lax.broadcasted_iota(jnp.int32, (128, 128), 0)
     left = lane < 64
     mine = span(c * 384, 384)
-    sems = iter(range(40))
+    sems = iter(range(60))
 
     def here(src, dst):
         copy = pltpu.make_async_copy(src, dst, loc.at[next(sems)])
         copy.start()
         return copy
+
+    reads = [here(a, b) for a, b in ((hidden_in, hidden), (upstream_in, upstream), (w_up_in, w_up), (w_down_in, w_down))]
 
     for k in range(4):
         columns = pl.ds(k * 128, 128)
         pieces = halves(w_qkv[1, :, columns], w_qkv[2, :, columns], left[:64])
         for j in (0, 1):
             shards[0, :, pl.ds(256 * k + 128 * j, 128)] = pieces[j].astype(BF)
-        shards[1, :, columns] = w_qkv[0, :, columns].astype(BF)
-        shards[1, :, pl.ds(512 + 128 * k, 128)] = w_dense[:, columns].astype(BF)
     net.greet(RING_XZ + FARTHER + (("x", 2),))
-    parts = [Gather(net, u, shards.at[u], gathered[u]) for u in range(PARTS)]
+    parts = [(FineGather if u < 2 else Gather)(net, u, shards.at[u], gathered[u]) for u in range(PARTS)]
     parts[0].begin(loc.at[next(sems)])
+    shards[1, :, LOW] = w_qkv[0].astype(BF)
+    shards[1, :, HIGH] = w_dense[...].astype(BF)
     parts[1].begin(loc.at[next(sems)])
-    for u in range(TILES):
-        shards[2 + u, :, LOW] = w_up[:, pl.ds(u * 512, 512)].astype(BF)
-        shards[2 + u, :, HIGH] = w_down[:, pl.ds(u * 512, 512)].astype(BF)
+    fill_tables(tables, near_cos, near_sin, base_cos, base_sin)
+    info[0:3] = jnp.where(keep[...] > 0, segments[...], -1)
+    info[3:6] = segments[...]
+    info[6:8] = jnp.zeros((2, 128), jnp.int32)
 
     def norm(t, carry):
         rows = span(t * 16, 16, 16)
@@ -415,6 +502,7 @@
         inputs[rows] = (value * gain[...] + shift[...]).astype(BF)
         return carry
 
+    reads[0].wait()
     lax.fori_loop(0, 24, norm, 0)
 
     def transpose(t, carry):
@@ -426,30 +514,49 @@
             staged[k, rows] = jnp.where(c == 0, second, first)
         return carry
 
-    lax.fori_loop(0, 16, transpose, 0)
     stays = []
-    for k, dst in enumerate((in_t, up_t)):
-        stays.append(here(kept.at[k], dst.at[c]))
-        net.push(("t", k), staged.at[k], dst.at[c], "s", 1)
+
+    def factors():
+        lax.fori_loop(0, 16, transpose, 0)
+        for k, dst in enumerate((in_t, up_t)):
+            stays.append(here(kept.at[k], dst.at[c]))
+            net.push(("t", k), staged.at[k], dst.at[c], "s", 1)
 
     def load(u):
         parts[u].landed()
         return here(gathered[u], weights.at[u % 4].reshape(4, 4, 2, 64, 1024))
 
-    for u in (0, 1):
-        parts[u].near()
+    first, second = parts[:2]
+    first.near()
+    first.pass_on(0)
+    second.near()
+    first.far()
+    second.pass_on(0)
+    reads[2].wait()
+    reads[3].wait()
+    for u in range(TILES):
+        shards[2 + u, :, LOW] = w_up[:, pl.ds(u * 512, 512)].astype(BF)
+        shards[2 + u, :, HIGH] = w_down[:, pl.ds(u * 512, 512)].astype(BF)
+    first.pass_on(-1)
+    first.pass_on(1)
+    second.far()
     parts[2].begin(loc.at[next(sems)])
-    for u in (0, 1):
-        parts[u].far()
-    for a in (0, -1, 1, 2):
-        for u in (0, 1):
-            parts[u].pass_on(a)
-    for a in (0, -1, 1, 2):
-        for u in (0, 1):
-            parts[u].close(a)
+    first.pass_on(2)
+    first.close(0)
+    second.pass_on(-1)
+    second.pass_on(1)
+    parts[3].begin(loc.at[next(sems)])
+    for a in (-1, 1, 2):
+        first.close(a)
+    second.pass_on(2)
     parts[2].near()
-    parts[3].begin(loc.at[next(sems)])
-    loads = {u: load(u) for u in (0, 1)}
+    parts[3].near()
+    loads = {0: load(0)}
+    second.close(0)
+    second.close(-1)
+    parts[4].begin(loc.at[next(sems)])
+    parts[5].begin(loc.at[next(sems)])
+    parts[2].far()
 
     loads[0].wait()
 
@@ -466,14 +573,18 @@
         return carry
 
     lax.fori_loop(0, 4, keys_values, 0)
+    pairs_of = kv_all.reshape(3, 8, 2, 128, 128)
     for dz, dx in OTHERS:
-        other = net.chip_at(dz, dx)
-        net.push(("k", dz, dx), kv.at[:, :, lanes(other)], kv_all.at[:, 2 * me + c], dz, dx)
         net.push(("i", dz, dx), info, info_all.at[2 * me + c], dz, dx)
-    net.push("ks", kv.at[:, :, lanes(me)], kv_all.at[:, 2 * me + c], "s", 1)
-    net.push("is", info, info_all.at[2 * me + c], "s", 1)
-    stays.append(here(kv.at[:, :, lanes(me)], kv_all.at[:, 2 * me + c]))
+    for s in range(3):
+        for dz, dx in OTHERS:
+            net.push(("k", s, dz, dx), kv.at[s, :, lanes(net.chip_at(dz, dx))], kv_all.at[s, 2 * me + c], dz, dx)
+        stays.append(here(kv.at[s, :, lanes(me)], kv_all.at[s, 2 * me + c]))
     stays.append(here(info, info_all.at[2 * me + c]))
+    second.close(1)
+    second.close(2)
+    loads[1] = load(1)
+    reads[1].wait()
     loads[1].wait()
 
     def queries(h, carry):
@@ -487,9 +598,10 @@
         return carry
 
     lax.fori_loop(0, 4, queries, 0)
-    for dz, dx in OTHERS:
-        net.push(("q", dz, dx), qd.at[:, :, lanes(net.chip_at(dz, dx))], qd_all.at[me], dz, dx)
-    stays.append(here(qd.at[:, :, lanes(me)], qd_all.at[me]))
+    for s in range(3):
+        for dz, dx in OTHERS:
+            net.push(("q", s, dz, dx), qd.at[s, :, lanes(net.chip_at(dz, dx))], qd_all.at[me, s], dz, dx)
+        stays.append(here(qd.at[s, :, lanes(me)], qd_all.at[me, s]))
 
     def units(u):
         slot = (2 + u) % 4
@@ -527,6 +639,8 @@
                 return carry
 
             lax.fori_loop(0, 4, spread, 0)
+            if u == TILES - 1:
+                stays.append(here(total_ref, share_out if total_ref is share else d_share_out))
 
     def attend(s, i, blocks, own, first):
         width = blocks * 128
@@ -560,82 +674,92 @@
         od[i, s] = jnp.where(left, back[:128] * (HD**-0.5), back[128:]).astype(BF)
         total[pl.ds(begin, width)] += dot(mixed, asking, ((0,), (0,)))
 
-    def sequence(s):
+    def early(s):
         total[...] = jnp.zeros_like(total)
         for i in range(4):
             attend(s, i, 2 * i + 2, 2 * i + c, 0)
 
-        def late(i, carry):
+    def late(s):
+        def some(i, carry):
             attend(s, i, 9, 2 * i + c, 2 * i + c - 8)
             return carry
 
-        lax.fori_loop(4, 8, late, 0)
+        lax.fori_loop(4, 8, some, 0)
         dkv[s] = total[...].astype(BF).reshape(8, 2, 128, 128)
 
-    parts[2].far()
-    for a in (0, -1, 1, 2):
-        parts[2].pass_on(a)
-    parts[3].near()
-    parts[4].begin(loc.at[next(sems)])
-    for a in (0, -1, 1, 2):
-        parts[2].close(a)
-    for dz, dx in OTHERS:
-        slot = 2 * net.chip_at(dz, -dx) + c
-        net.arrived(("k", dz, dx))
-        net.push(("ks", dz, dx), kv_all.at[:, slot], kv_all.at[:, slot], "s", 1)
-        net.arrived(("i", dz, dx))
-        net.push(("is", dz, dx), info_all.at[slot], info_all.at[slot], "s", 1)
-    parts[3].far()
-    loads[2] = load(2)
-    for a in (0, -1, 1, 2):
-        parts[3].pass_on(a)
+    def relay(s):
+        for dz, dx in OTHERS:
+            net.arrived(("k", s, dz, dx))
+        held = pairs_of.at[s, :, c]
+        net.push(("ks", s), held, held, "s", 1)
+
+    def ready(s):
+        net.arrived(("ks", s))
+        for dz, dx in OTHERS:
+            net.arrived(("q", s, dz, dx))
+
+    def give(s):
+        net.push(("b", s), dkv.at[s, :, 1 - c], theirs.at[s], "s", 1)
+        stays.append(here(od.at[me, s], od_in.at[s, :, lanes(me)]))
+        for dz, dx in OTHERS:
+            net.push(("o", s, dz, dx), od.at[net.chip_at(dz, dx), s], od_in.at[s, :, lanes(me)], dz, dx)
+
+    def give_more(s):
+        net.arrived(("b", s))
+        ours[s] = dkv[s, :, c] + theirs[s]
+        for dz, dx in OTHERS:
+            net.push(("d", s, dz, dx), ours.at[s, net.chip_at(dz, dx)], dkv_in.at[s, :, lanes(me)], dz, dx)
+        stays.append(here(ours.at[s, me], dkv_in.at[s, :, lanes(me)]))
+
     parts[4].near()
-    parts[5].begin(loc.at[next(sems)])
-    for dz, dx in OTHERS:
-        for kind in ("q", "ks", "is"):
-            net.arrived((kind, dz, dx))
-    net.arrived("ks")
-    net.arrived("is")
+    parts[5].near()
+    factors()
+    parts[2].pass_on()
     for copy in stays:
         copy.wait()
     stays.clear()
+    for dz, dx in OTHERS:
+        net.arrived(("i", dz, dx))
+    held_info = info_all.reshape(8, 2, 8, 128).at[:, c]
+    net.push("is", held_info, held_info, "s", 1)
+    relay(0)
+    relay(1)
+    relay(2)
+    net.arrived("is")
     for b in range(16):
         seen[:, b * 128 : (b + 1) * 128] = info_all[b]
-    sequence(0)
-    for a in (0, -1, 1, 2):
-        parts[3].close(a)
+    parts[3].far()
+    parts[2].close()
+    ready(0)
+    early(0)
+    parts[3].pass_on()
+    late(0)
+    give(0)
     parts[4].far()
-    for a in (0, -1, 1):
-        parts[4].pass_on(a)
-    parts[5].near()
-    parts[4].pass_on(2)
-    sequence(1)
+    loads[2] = load(2)
+    units(0)
+    ready(1)
+    parts[3].close()
+    early(1)
+    parts[4].pass_on()
+    give_more(0)
     parts[5].far()
-    for a in (0, -1, 1, 2):
-        parts[4].close(a)
-    for a in (0, -1, 1):
-        parts[5].pass_on(a)
-    sequence(2)
-    net.push("b", dkv.at[:, :, 1 - c], theirs, "s", 1)
-    mixed = here(dkv.at[:, :, c], ours)
-    stays.append(here(od.at[me], od_in.at[:, :, lanes(me)]))
-    for dz, dx in OTHERS:
-        net.push(("o", dz, dx), od.at[net.chip_at(dz, dx)], od_in.at[:, :, lanes(me)], dz, dx)
-    mixed.wait()
-    net.arrived("b")
-    ours[...] = ours[...] + theirs[...]
-    for dz, dx in OTHERS:
-        net.push(("d", dz, dx), ours.at[:, net.chip_at(dz, dx)], dkv_in.at[:, :, lanes(me)], dz, dx)
-    stays.append(here(ours.at[:, me], dkv_in.at[:, :, lanes(me)]))
-    parts[5].pass_on(2)
-    for a in (0, -1, 1, 2):
-        parts[5].close(a)
+    late(1)
+    give(1)
     loads[3] = load(3)
+    units(1)
+    ready(2)
+    parts[4].close()
+    early(2)
+    parts[5].pass_on()
+    give_more(1)
+    late(2)
+    give(2)
     loads[4] = load(4)
-    units(0)
-    units(1)
+    parts[5].close()
+    give_more(2)
+    units(2)
     loads[5] = load(5)
-    units(2)
     units(3)
     for copy in stays:
         copy.wait()
@@ -652,8 +776,8 @@
         out_shape=[big] * PARTS
         + [factor, factor, jax.ShapeDtypeStruct((TILES, 768, 1024), BF), heads, heads]
         + [wide, wide, jax.ShapeDtypeStruct((1, 2048), F32)],
-        in_specs=[VMEM] * len(args),
-        out_specs=[ANY] * (PARTS + 5) + [VMEM] * 3,
+        in_specs=[ANY] * 4 + [VMEM] * (len(args) - 4),
+        out_specs=[ANY] * (PARTS + 7) + [VMEM],
         scratch_shapes=[
             pltpu.VMEM((PARTS, 64, 1024), BF),
             pltpu.VMEM((384, 2048), BF),
@@ -672,9 +796,19 @@
             pltpu.VMEM((3, 8, 128, 128), BF),
             pltpu.VMEM((3, 8, 128, 128), BF),
             pltpu.VMEM((TILES, 384, 1024), BF),
-            pltpu.SemaphoreType.DMA((540,)),
-            pltpu.SemaphoreType.DMA((540,)),
-            pltpu.SemaphoreType.DMA((40,)),
+            pltpu.VMEM((384, 2048), F32),
+            pltpu.VMEM((384, 2048), F32),
+            pltpu.VMEM((384, 2048), BF),
+            pltpu.VMEM((384, 2048), BF),
+            pltpu.VMEM((64, 2048), F32),
+            pltpu.VMEM((64, 2048), F32),
+            pltpu.VMEM((8, 128), jnp.int32),
+            pltpu.VMEM((128, 128), F32),
+            pltpu.VMEM((128, 128), F32),
+            pltpu.VMEM((128, 128), F32),
+            pltpu.SemaphoreType.DMA((370,)),
+            pltpu.SemaphoreType.DMA((370,)),
+            pltpu.SemaphoreType.DMA((60,)),
         ],
         compiler_params=pltpu.CompilerParams(
             collective_id=cid, has_side_effects=True, vmem_limit_bytes=62 * 2**20
@@ -684,13 +818,13 @@
 
 
 def back_kernel(
-    od_in, dkv_in, upstream, hidden, in_t, up_t, pairs, heads_w0, heads_w1, share_in, d_share_in, bias_up, gain, t_cos,
-    t_low, t_high, input_grad, sum0, sum1, done, vec_out, *refs,
+    od_in, dkv_in, upstream, hidden, in_t, up_t, pairs, heads_w0, heads_w1, share_in, d_share_in, bias_up, gain, near_cos,
+    near_sin, base_cos, base_sin, input_grad, sum0, sum1, done, vec_out, *refs,
 ):
     accs, refs = refs[:PARTS], refs[PARTS:]
     far1, near1, far2, near2, refs = *refs[:4], refs[4:]
     weights, pair, factors, share, d_share, refs = *refs[:5], refs[5:]
-    y_far, y_near, vecs, vec_acc, cores, alongx, alongz, alongy, send, recv, loc = refs
+    y_far, y_near, vecs, vec_acc, cores, alongx, alongz, alongy, t_cos, t_low, t_high, send, recv, loc = refs
     net = Net(send, recv)
     c = net.c
     tables = (t_cos, t_low, t_high)
@@ -712,6 +846,8 @@
         Scatter(net, ("g", i), accs[i], far1.at[i], near1.at[i], far2.at[i], near2.at[i], done.at[i])
         for i in range(PARTS)
     ]
+
+    fill_tables(tables, near_cos, near_sin, base_cos, base_sin)
 
     def rows_of(s, carry):
         own = span(c * 384 + s * 128, 128)
@@ -878,7 +1014,7 @@
         out_shape=[wide]
         + [jax.ShapeDtypeStruct((4, 192, 1024), BF)] * 2
         + [jax.ShapeDtypeStruct((PARTS, 64, 1024), F32), jax.ShapeDtypeStruct((8, 2048), F32)],
-        in_specs=[VMEM] * 4 + [ANY] * 7 + [VMEM] * 5,
+        in_specs=[VMEM] * 4 + [ANY] * 7 + [VMEM] * 6,
         out_specs=[ANY] * 3 + [VMEM] * 2,
         scratch_shapes=[pltpu.VMEM((4, 4, 64, 1024), BF)] * PARTS
         + [
@@ -899,6 +1035,9 @@
             pltpu.VMEM((4, 8, 2048), F32),
             pltpu.VMEM((4, 8, 2048), F32),
             pltpu.VMEM((4, 8, 2048), F32),
+            pltpu.VMEM((128, 128), F32),
+            pltpu.VMEM((128, 128), F32),
+            pltpu.VMEM((128, 128), F32),
             pltpu.SemaphoreType.DMA((140,)),
             pltpu.SemaphoreType.DMA((140,)),
             pltpu.SemaphoreType.DMA((40,)),
@@ -977,24 +1116,16 @@
     cotangent,
 ):
     rows, width = 384, 2048
-    positions = lax.axis_index("seq") * 128 + jnp.arange(128, dtype=jnp.int32)
-    half = ROT // 2
-    frequency = 10000.0 ** (-(jnp.arange(half, dtype=F32) * 2.0) / ROT)
-    quiet = jnp.zeros((HD - ROT,), F32)
-    places = jnp.arange(128, dtype=jnp.int32) % HD
-    turned = positions.astype(F32)[:, None] * jnp.concatenate([frequency, frequency, quiet] * 2)[None, :]
-    t_cos = jnp.cos(turned)
-    t_low = jnp.where(places < half, jnp.sin(turned), 0.0)
-    t_high = jnp.where(places >= half, jnp.sin(turned), 0.0)
-    tables = [t_cos, t_low, t_high]
-    info = jnp.concatenate(
-        [jnp.where(keep_mask > 0, segments, -1), segments, jnp.zeros((2, 128), jnp.int32)], axis=0
-    )
+    lanes_of = np.arange(128) % HD
+    frequency = np.float32(10000.0) ** (-(np.arange(ROT // 2, dtype=np.float32) * 2.0) / ROT)
+    frequency = np.where(lanes_of < ROT, np.resize(frequency.astype(np.float64), 128), 0.0)
+    near, base = np.arange(128)[:, None] * frequency, 128 * np.arange(16)[:, None] * frequency
+    tables = [jnp.asarray(t.astype(np.float32)) for t in (np.cos(near), np.sin(near), np.cos(base), np.sin(base))]
     hidden = hidden_in.reshape(rows, width)
     upstream = cotangent.reshape(rows, width)
     outs = forward(
-        [hidden, upstream, ln_gain[None], ln_shift[None], w_qkv.transpose(1, 0, 2), b_qkv, w_dense.T, w_up]
-        + [b_up[None], w_down.T, info, *tables],
+        [hidden, upstream, w_up, w_down.T, ln_gain[None], ln_shift[None], w_qkv.transpose(1, 0, 2), b_qkv, w_dense.T]
+        + [b_up[None], segments, keep_mask, *tables],
         0,
     )
     heads_w = [w.reshape(2048, 1024) for w in outs[:2]]

time: 265 us -> 235 us (0.89)
  Pallas kernels: 260 us -> 233 us
  other arithmetic: 3.06 us -> 0 us
    pallas_call x1, Pallas kernels: 159 us -> 132 us  [forward(): pl.pallas_call(front_kernel, out_shape=[big] * PARTS + [factor, factor, j...]
where the time goes in v1:
time: 235 us; the launch traced here: 234 us
  Pallas kernels  233 us (99%)
    pallas_call x1, Pallas kernels, forward(): pl.pallas_call(front_kernel, out_shape=[big] * PARTS + [factor, factor, j...  132 us
    pallas_call x1, Pallas kernels, backward(): pl.pallas_call(back_kernel, out_shape=[wide] + [jax.ShapeDtypeStruct((4,...  93.8 us
    pallas_call x1, Pallas kernels, finish(): pl.pallas_call(finish_kernel, grid=(4,), out_shape=[wide, wide] + small,...  7.32 us

profile of v1, /device:TPU:0, one launch (start us, length us, event | category | flops | bytes accessed | tf_op | source)
XLA Modules:
  0.0 234.3 jit_solution(5718753444166401906)
XLA Ops:
  0.6 132.3 %forward.1 = (bf16[4,4,2,64,1024]{4,3,2,1,0:T(8,128)(2,1)}, bf16[4,4,2,64,1024]{4,3,2,1,0:T(8,128)(2,1)}, bf16[4,4,2,64,1024]{4,3,2,1,0:T(8,128)(2,1)}, bf16[4,4...) custom-call(bf16[384,2048]{1,0:T(8,128)(2,1)} %bitcast.17, ...), custom_call_target="tpu_custom_call" | custom-call | tf_op jit(solution)/shard_map/forward/pallas_call | solution.py:774
  133.0 93.8 %backward.1 = (f32[384,2048]{1,0:T(8,128)}, bf16[4,192,1024]{2,1,0:T(8,128)(2,1)}, bf16[4,192,1024]{2,1,0:T(8,128)(2,1)}, f32[6,64,1024]{2,1,0:T(8,128)}, f32[8,2048]{1,0:T(8,128)}) custom-call(bf16[3,128,1024]{2,1,0:T(8,128)(2,1)} %get-tuple-element.38.od_in, bf16[3,128,1024]{2,1,0:T(8,128)(2,1)} %get-tuple-element.39.dkv_in, bf16[384,2048]{1,0:T(8,128)(2,1)} %bitcast.21, ...), custom_call_target="tpu_custom_call" | custom-call | tf_op jit(solution)/shard_map/backward/pallas_call | solution.py:1012
  226.8 7.3 %finish.1 = (f32[384,2048]{1,0:T(8,128)}, f32[384,2048]{1,0:T(8,128)}, f32[3,64,512]{2,1,0:T(8,128)}, f32[64,512]{1,0:T(8,128)}, f32[64,2048]{1,0:T(8,128)}, /*i...) custom-call(bf16[384,2048]{1,0:T(8,128)(2,1)} %bitcast.19, ...), custom_call_target="tpu_custom_call" | custom-call | tf_op jit(solution)/shard_map/finish/pallas_call | solution.py:1102

commit v2 on v1

--- a/solution.py
+++ b/solution.py
@@ -81,6 +81,10 @@
     def sent(self, key):
         self.out.pop(key).wait_send()
 
+    def settle(self, keep=0):
+        for key in list(self.out)[: len(self.out) - keep]:
+            self.sent(key)
+
     def drain(self):
         for key in list(self.out):
             self.sent(key)
@@ -107,6 +111,7 @@
 OTHERS = tuple((dz, dx) for dz in (1, 0) for dx in (2, 1, 3, 0) if dz or dx)
 PARTS = 6
 TILES = 4
+EARLY = 3
 LOW, HIGH, ALL = pl.ds(0, 512), pl.ds(512, 512), pl.ds(0, 1024)
 
 
@@ -261,6 +266,15 @@
             for a in (0, -1, 1, 2):
                 for b in (-1, 1, 2):
                     n.arrived((self.name, h, "s", a, b))
+
+
+def gelu_both(v, d):
+    k = 0.7978845608028654
+    square = v * v
+    t = jnp.tanh(k * v * (1.0 + 0.044715 * square))
+    half = 0.5 * (1.0 + t)
+    slope = half + 0.5 * v * (1.0 - t * t) * (k * (1.0 + 0.134145 * square))
+    return (d * slope).astype(BF), (v * half).astype(BF)
 
 
 def fill_tables(tables, near_cos, near_sin, base_cos, base_sin):
@@ -458,7 +472,7 @@
     near_cos, near_sin, base_cos, base_sin, *refs,
 ):
     gathered, refs = refs[:PARTS], refs[PARTS:]
-    in_t, up_t, pairs, od_in, dkv_in, share_out, d_share_out, bias_up, refs = *refs[:8], refs[8:]
+    in_t, up_t, pairs, od_in, dkv_in, inputs_out, share_out, d_share_out, bias_up, refs = *refs[:9], refs[9:]
     shards, inputs, staged, kept, weights, qd, kv, qd_all, kv_all, info_all, seen, total, refs = *refs[:12], refs[12:]
     od, dkv, theirs, ours, pair, share, d_share, hidden, upstream, w_up, w_down, info, refs = *refs[:12], refs[12:]
     t_cos, t_low, t_high, send, recv, loc = refs
@@ -514,7 +528,7 @@
             staged[k, rows] = jnp.where(c == 0, second, first)
         return carry
 
-    stays = []
+    stays = [here(inputs, inputs_out)]
 
     def factors():
         lax.fori_loop(0, 16, transpose, 0)
@@ -612,14 +626,9 @@
             unit = span(u * 512 + j * 256, 256)
             v = dot(inputs[...], weights[slot, :, low], ((1,), (0,))) + b_up[:, unit]
             d = dot(upstream[...], weights[slot, :, high], ((1,), (0,)))
-            k = 0.7978845608028654
-            square = v * v
-            t = jnp.tanh(k * v * (1.0 + 0.044715 * square))
-            half = 0.5 * (1.0 + t)
-            slope = half + 0.5 * v * (1.0 - t * t) * (k * (1.0 + 0.134145 * square))
-            d_up = (d * slope).astype(BF)
+            d_up, active = gelu_both(v, d)
             pair[u, :, low] = d_up
-            pair[u, :, high] = (v * half).astype(BF)
+            pair[u, :, high] = active
             bias_up[:, unit] = jnp.sum(d_up.astype(F32), axis=0, keepdims=True)
             return carry
 
@@ -639,7 +648,7 @@
                 return carry
 
             lax.fori_loop(0, 4, spread, 0)
-            if u == TILES - 1:
+            if u == EARLY - 1:
                 stays.append(here(total_ref, share_out if total_ref is share else d_share_out))
 
     def attend(s, i, blocks, own, first):
@@ -730,6 +739,7 @@
         seen[:, b * 128 : (b + 1) * 128] = info_all[b]
     parts[3].far()
     parts[2].close()
+    net.settle(60)
     ready(0)
     early(0)
     parts[3].pass_on()
@@ -738,6 +748,7 @@
     parts[4].far()
     loads[2] = load(2)
     units(0)
+    net.settle(50)
     ready(1)
     parts[3].close()
     early(1)
@@ -748,6 +759,7 @@
     give(1)
     loads[3] = load(3)
     units(1)
+    net.settle(50)
     ready(2)
     parts[4].close()
     early(2)
@@ -756,11 +768,11 @@
     late(2)
     give(2)
     loads[4] = load(4)
+    net.settle(40)
     parts[5].close()
     give_more(2)
     units(2)
-    loads[5] = load(5)
-    units(3)
+    parts[5].landed()
     for copy in stays:
         copy.wait()
     net.drain()
@@ -774,10 +786,11 @@
     return pl.pallas_call(
         front_kernel,
         out_shape=[big] * PARTS
-        + [factor, factor, jax.ShapeDtypeStruct((TILES, 768, 1024), BF), heads, heads]
+        + [factor, factor, jax.ShapeDtypeStruct((EARLY, 768, 1024), BF), heads, heads]
+        + [jax.ShapeDtypeStruct((384, 2048), BF)]
         + [wide, wide, jax.ShapeDtypeStruct((1, 2048), F32)],
         in_specs=[ANY] * 4 + [VMEM] * (len(args) - 4),
-        out_specs=[ANY] * (PARTS + 7) + [VMEM],
+        out_specs=[ANY] * (PARTS + 8) + [VMEM],
         scratch_shapes=[
             pltpu.VMEM((PARTS, 64, 1024), BF),
             pltpu.VMEM((384, 2048), BF),
@@ -795,7 +808,7 @@
             pltpu.VMEM((3, 8, 2, 128, 128), BF),
             pltpu.VMEM((3, 8, 128, 128), BF),
             pltpu.VMEM((3, 8, 128, 128), BF),
-            pltpu.VMEM((TILES, 384, 1024), BF),
+            pltpu.VMEM((EARLY, 384, 1024), BF),
             pltpu.VMEM((384, 2048), F32),
             pltpu.VMEM((384, 2048), F32),
             pltpu.VMEM((384, 2048), BF),
@@ -818,12 +831,13 @@
 
 
 def back_kernel(
-    od_in, dkv_in, upstream, hidden, in_t, up_t, pairs, heads_w0, heads_w1, share_in, d_share_in, bias_up, gain, near_cos,
+    od_any, dkv_any, upstream_any, hidden_any, in_t, up_t, pairs, heads_w0, heads_w1, last_w,
+    inputs_any, share_in, d_share_in, bias_up, b_up, gain, near_cos,
     near_sin, base_cos, base_sin, input_grad, sum0, sum1, done, vec_out, *refs,
 ):
     accs, refs = refs[:PARTS], refs[PARTS:]
     far1, near1, far2, near2, refs = *refs[:4], refs[4:]
-    weights, pair, factors, share, d_share, refs = *refs[:5], refs[5:]
+    weights, pair, factors, share, d_share, od_in, dkv_in, upstream, hidden, inputs, refs = *refs[:10], refs[10:]
     y_far, y_near, vecs, vec_acc, cores, alongx, alongz, alongy, t_cos, t_low, t_high, send, recv, loc = refs
     net = Net(send, recv)
     c = net.c
@@ -838,9 +852,13 @@
         return copy
 
     factor_loads = [here(src.at[k], factors.at[j, :, pl.ds(384 * k, 384)]) for j, src in enumerate((in_t, up_t)) for k in (0, 1)]
-    pair_loads = {u: here(pairs.at[u], pair.at[u]) for u in (0, 1)}
-    weight_loads = [here(src, weights.at[k]) for k, src in enumerate((heads_w0, heads_w1))]
+    pair_loads = {0: here(pairs.at[0], pair.at[0])}
+    head_loads = [here(od_any, od_in), here(dkv_any, dkv_in)]
+    unit_loads = [here(last_w, weights.at[0]), here(inputs_any, inputs), here(upstream_any, upstream)]
+    pair_loads[1] = here(pairs.at[1], pair.at[1])
     share_loads = [here(d_share_in, d_share), here(share_in, share)]
+    weight_loads = [here(heads_w1, weights.at[1])]
+    row_loads = [here(hidden_any, hidden)]
     net.greet(RING_XZ + RING_Y + FAR)
     parts = [
         Scatter(net, ("g", i), accs[i], far1.at[i], near1.at[i], far2.at[i], near2.at[i], done.at[i])
@@ -863,10 +881,13 @@
             pair[3, own, pl.ds(512 + h * 128, 128)] = got.astype(BF)
         return carry
 
-    lax.fori_loop(0, 3, rows_of, 0)
-    for slot in (2, 3):
-        rows = pair.at[slot, mine]
-        net.push(("p", slot), rows, rows, "s", 1)
+    def heads():
+        for copy in head_loads:
+            copy.wait()
+        lax.fori_loop(0, 3, rows_of, 0)
+        for slot in (2, 3):
+            rows = pair.at[slot, mine]
+            net.push(("p", slot), rows, rows, "s", 1)
 
     def gradients(u, slot, first_t, second_t):
         acc = accs[u]
@@ -885,18 +906,39 @@
     def tile(u):
         pair_loads[u].wait()
         gradients(u, u % 2, 0, 1)
-        if u + 2 < TILES:
+        if u + 2 < EARLY:
             pair_loads[u + 2] = here(pairs.at[u + 2], pair.at[u % 2])
 
-    def spread(total, slot, columns):
+    def spread(total, slot, source, columns):
         value = pair[slot, mine, columns]
 
         def chunk(j, carry):
             rows = span(j * 512, 512)
-            total[:, rows] += dot(value, weights[slot - 2, rows, columns], ((1,), (1,)))
+            total[:, rows] += dot(value, weights[source, rows, columns], ((1,), (1,)))
             return carry
 
         lax.fori_loop(0, 4, chunk, 0)
+
+    def units():
+        for copy in unit_loads + share_loads:
+            copy.wait()
+
+        def some(j, carry):
+            low, high = span(j * 256, 256), span(512 + j * 256, 256)
+            unit = span(EARLY * 512 + j * 256, 256)
+            v = dot(inputs[...], weights[0, :, low], ((1,), (0,))) + b_up[:, unit]
+            d = dot(upstream[...], weights[0, :, high], ((1,), (0,)))
+            d_up, active = gelu_both(v, d)
+            pair[4, mine, low] = d_up
+            pair[4, mine, high] = active
+            return carry
+
+        lax.fori_loop(0, 2, some, 0)
+        rows = pair.at[4, mine]
+        net.push(("p", 4), rows, rows, "s", 1)
+        spread(d_share, 4, 0, LOW)
+        spread(share, 4, 0, HIGH)
+        weight_loads.append(here(heads_w0, weights.at[0]))
 
     def normed(rows):
         value = hidden[rows].astype(F32)
@@ -919,7 +961,8 @@
         lax.fori_loop(0, 24, chunk, 0)
         for k in range(3):
             vecs[k : k + 1] = jnp.sum(vec_acc[k], axis=0, keepdims=True)
-        vecs[3:4] = bias_up[...]
+        vecs[3:4, 0 : EARLY * 512] = bias_up[:, 0 : EARLY * 512]
+        vecs[3:4, EARLY * 512 : 2048] = jnp.sum(pair[4, mine, LOW].astype(F32), axis=0, keepdims=True)
         for k in range(4):
             columns = pl.ds(k * 256, 256)
             vecs[4:5, columns] = jnp.sum(pair[2, mine, columns].astype(F32), axis=0, keepdims=True)
@@ -946,63 +989,67 @@
     for copy in factor_loads:
         copy.wait()
     tile(0)
+    heads()
     tile(1)
-    for copy in weight_loads + share_loads:
-        copy.wait()
-    spread(d_share, 2, ALL)
-    spread(d_share, 3, LOW)
+    parts[0].step3()
+    units()
+    parts[1].step3()
+    weight_loads[0].wait()
+    spread(d_share, 3, 1, LOW)
+    parts[0].step4()
+    weight_loads[1].wait()
+    spread(d_share, 2, 0, ALL)
     ys[0].step1(d_share)
-    spread(share, 3, HIGH)
+    parts[1].step4()
+    spread(share, 3, 1, HIGH)
     ys[1].step1(share)
-    parts[0].step3()
+    tile(2)
+    parts[0].step5()
+    ys[0].step2()
+    net.arrived(("p", 4))
+    gradients(3, 4, 0, 1)
+    parts[2].step3()
+    parts[1].step5()
+    ys[1].step2()
+    row_loads[0].wait()
+    vectors()
+    vec = vector_sum(net, vecs, cores, alongx, alongz, alongy, vec_out)
+    next(vec)
+    parts[3].step3()
+    parts[0].step6()
+    parts[2].step4()
+    ys[0].step3(loc.at[next(sems)])
     for slot in (2, 3):
         net.arrived(("p", slot))
     gradients(4, 2, 0, 0)
-    ys[0].step2()
-    parts[1].step3()
+    next(vec)
+    parts[3].step4()
+    parts[1].step6()
+    parts[2].step5()
+    ys[1].step3(loc.at[next(sems)])
     gradients(5, 3, 0, 1)
-    ys[1].step2()
-    vectors()
-    vec = vector_sum(net, vecs, cores, alongx, alongz, alongy, vec_out)
     next(vec)
-    parts[0].step4()
-    ys[0].step3(loc.at[next(sems)])
-    tile(2)
     parts[4].step3()
-    parts[1].step4()
+    parts[3].step5()
+    ys[0].step4()
+    parts[5].step3()
     next(vec)
-    ys[1].step3(loc.at[next(sems)])
-    tile(3)
-    parts[0].step5()
-    parts[5].step3()
-    ys[0].step4()
     parts[4].step4()
-    next(vec)
-    parts[1].step5()
-    parts[0].step6()
-    parts[2].step3()
+    parts[2].step6()
     ys[1].step4()
     parts[5].step4()
+    parts[3].step6()
     next(vec)
     parts[4].step5()
-    parts[1].step6()
-    parts[3].step3()
     ys[0].step5()
     got0 = here(sum0, weights.at[1, pl.ds(0, 768)].reshape(4, 192, 1024))
-    parts[2].step4()
-    next(vec)
     parts[5].step5()
-    parts[4].step6()
     got0.wait()
     finish_in()
     out0 = here(d_share, input_grad)
-    parts[3].step4()
-    parts[2].step5()
+    parts[4].step6()
+    ys[1].step5()
     parts[5].step6()
-    ys[1].step5()
-    parts[3].step5()
-    parts[2].step6()
-    parts[3].step6()
     out0.wait()
     net.drain()
 
@@ -1014,7 +1061,7 @@
         out_shape=[wide]
         + [jax.ShapeDtypeStruct((4, 192, 1024), BF)] * 2
         + [jax.ShapeDtypeStruct((PARTS, 64, 1024), F32), jax.ShapeDtypeStruct((8, 2048), F32)],
-        in_specs=[VMEM] * 4 + [ANY] * 7 + [VMEM] * 6,
+        in_specs=[ANY] * 13 + [VMEM] * 7,
         out_specs=[ANY] * 3 + [VMEM] * 2,
         scratch_shapes=[pltpu.VMEM((4, 4, 64, 1024), BF)] * PARTS
         + [
@@ -1023,10 +1070,15 @@
             pltpu.VMEM((PARTS, 2, 2, 16, 1024), BF),
             pltpu.VMEM((PARTS, 2, 2, 32, 1024), BF),
             pltpu.VMEM((2, 2048, 1024), BF),
-            pltpu.VMEM((4, 768, 1024), BF),
+            pltpu.VMEM((5, 768, 1024), BF),
             pltpu.VMEM((2, 1024, 768), BF),
             pltpu.VMEM((384, 2048), F32),
             pltpu.VMEM((384, 2048), F32),
+            pltpu.VMEM((3, 128, 1024), BF),
+            pltpu.VMEM((3, 128, 1024), BF),
+            pltpu.VMEM((384, 2048), BF),
+            pltpu.VMEM((384, 2048), BF),
+            pltpu.VMEM((384, 2048), BF),
             pltpu.VMEM((2, 2, 96, 1024), BF),
             pltpu.VMEM((2, 2, 192, 1024), BF),
             pltpu.VMEM((8, 2048), F32),
@@ -1128,10 +1180,12 @@
         + [b_up[None], segments, keep_mask, *tables],
         0,
     )
-    heads_w = [w.reshape(2048, 1024) for w in outs[:2]]
-    in_t, up_t, pairs, od_in, dkv_in, share, d_share, bias_up = outs[PARTS:]
+    heads_w = [outs[u].reshape(2048, 1024) for u in (0, 1, PARTS - 1)]
+    in_t, up_t, pairs, od_in, dkv_in, inputs, share, d_share, bias_up = outs[PARTS:]
     input_grad, _, summed, done, vectors = backward(
-        [od_in, dkv_in, upstream, hidden, in_t, up_t, pairs, *heads_w, share, d_share, bias_up, ln_gain[None], *tables], 1
+        [od_in, dkv_in, upstream, hidden, in_t, up_t, pairs, *heads_w, inputs, share, d_share, bias_up]
+        + [b_up[None], ln_gain[None], *tables],
+        1,
     )
     block_out, input_grad, grad_qkv, grad_dense, grad_up, grad_down, gain, shift, out, up, grad_bqkv, out2 = finish(
         hidden, summed, b_dense[None], b_down[None], input_grad, done, vectors

time: 235 us -> 227 us (0.966)
  Pallas kernels: 233 us -> 225 us
    pallas_call x1, Pallas kernels: 132 us -> 124 us  [forward(): pl.pallas_call(front_kernel, out_shape=[big] * PARTS + [factor, factor, j...]
where the time goes in v2:
time: 227 us; the launch traced here: 226 us
  Pallas kernels  225 us (99%)
    pallas_call x1, Pallas kernels, forward(): pl.pallas_call(front_kernel, out_shape=[big] * PARTS + [factor, factor, j...  124 us
    pallas_call x1, Pallas kernels, backward(): pl.pallas_call(back_kernel, out_shape=[wide] + [jax.ShapeDtypeStruct((4,...  94.3 us
    pallas_call x1, Pallas kernels, finish(): pl.pallas_call(finish_kernel, grid=(4,), out_shape=[wide, wide] + small,...  7.32 us

profile of v2, /device:TPU:0, one launch (start us, length us, event | category | flops | bytes accessed | tf_op | source)
XLA Modules:
  0.0 226.2 jit_solution(9044729197123435487)
XLA Ops:
  0.6 123.8 %forward.1 = (bf16[4,4,2,64,1024]{4,3,2,1,0:T(8,128)(2,1)}, bf16[4,4,2,64,1024]{4,3,2,1,0:T(8,128)(2,1)}, bf16[4,4,2,64,1024]{4,3,2,1,0:T(8,128)(2,1)}, bf16[4,4...) custom-call(bf16[384,2048]{1,0:T(8,128)(2,1)} %bitcast.18, ...), custom_call_target="tpu_custom_call" | custom-call | tf_op jit(solution)/shard_map/forward/pallas_call | solution.py:786
  124.4 94.3 %backward.1 = (f32[384,2048]{1,0:T(8,128)}, bf16[4,192,1024]{2,1,0:T(8,128)(2,1)}, bf16[4,192,1024]{2,1,0:T(8,128)(2,1)}, f32[6,64,1024]{2,1,0:T(8,128)}, f32[8,2048]{1,0:T(8,128)}) custom-call(bf16[3,128,1024]{2,1,0:T(8,128)(2,1)} %get-tuple-element.40.od_any, bf16[3,128,1024]{2,1,0:T(8,128)(2,1)} %get-tuple-element.41.dkv_any, bf16[384,2048]{1,0:T(8,128)(2,1)} %bitcast.22, ...), custom_call_target="tpu_custom_call" | custom-call | tf_op jit(solution)/shard_map/backward/pallas_call | solution.py:1059
  218.7 7.3 %finish.1 = (f32[384,2048]{1,0:T(8,128)}, f32[384,2048]{1,0:T(8,128)}, f32[3,64,512]{2,1,0:T(8,128)}, f32[64,512]{1,0:T(8,128)}, f32[64,2048]{1,0:T(8,128)}, /*i...) custom-call(bf16[384,2048]{1,0:T(8,128)(2,1)} %bitcast.20, ...), custom_call_target="tpu_custom_call" | custom-call | tf_op jit(solution)/shard_map/finish/pallas_call | solution.py:1154

commit v3 on v2

--- a/solution.py
+++ b/solution.py
@@ -1108,8 +1108,10 @@
     for half in (0, 1):
         columns = pl.ds(half * 1024, 1024)
         bias = b_dense[:, columns] + b_down[:, columns]
-        got = summed[0, pl.ds(96 * half, 96)].astype(F32)
-        block_out[:, columns] = hidden[:, columns].astype(F32) + got + bias
+        for d in (0, 1):
+            rows = pl.ds(96 * d, 96)
+            got = summed[d, pl.ds(96 * half, 96)].astype(F32)
+            block_out[rows, columns] = hidden[rows, columns].astype(F32) + got + bias
     input_grad[...] = grad[...]
 
     @pl.when(pl.program_id(0) == 0)
@@ -1134,7 +1136,7 @@
 
 def finish(hidden, summed, b_dense, b_down, grad, done, vecs):
     wide, row = jax.ShapeDtypeStruct((384, 2048), F32), jax.ShapeDtypeStruct((2048,), F32)
-    rows = pl.BlockSpec((96, 2048), lambda i: (i, 0))
+    rows = pl.BlockSpec((192, 2048), lambda i: (i, 0))
     small = [
         jax.ShapeDtypeStruct((3, 64, 512), F32),
         jax.ShapeDtypeStruct((64, 512), F32),
@@ -1153,9 +1155,9 @@
 
     return pl.pallas_call(
         finish_kernel,
-        grid=(4,),
+        grid=(2,),
         out_shape=[wide, wide] + small,
-        in_specs=[rows, pl.BlockSpec((1, 192, 1024), lambda i: (i, 0, 0)), whole((1, 2048)), whole((1, 2048)), rows]
+        in_specs=[rows, pl.BlockSpec((2, 192, 1024), lambda i: (i, 0, 0)), whole((1, 2048)), whole((1, 2048)), rows]
         + [whole((PARTS, 64, 1024)), whole((8, 2048))],
         out_specs=[rows, rows] + [whole(s.shape) for s in small],
         compiler_params=pltpu.CompilerParams(vmem_limit_bytes=62 * 2**20),

time: 227 us -> 226 us (level)
  no operation moved by 1% of the time
where the time goes in v3:
time: 226 us; the launch traced here: 225 us
  Pallas kernels  224 us (99%)
    pallas_call x1, Pallas kernels, forward(): pl.pallas_call(front_kernel, out_shape=[big] * PARTS + [factor, factor, j...  124 us
    pallas_call x1, Pallas kernels, backward(): pl.pallas_call(back_kernel, out_shape=[wide] + [jax.ShapeDtypeStruct((4,...  94.3 us
    pallas_call x1, Pallas kernels, finish(): pl.pallas_call(finish_kernel, grid=(2,), out_shape=[wide, wide] + small,...  6.36 us

profile of v3, /device:TPU:0, one launch (start us, length us, event | category | flops | bytes accessed | tf_op | source)
XLA Modules:
  0.0 225.2 jit_solution(17832366985615035061)
XLA Ops:
  0.6 123.8 %forward.1 = (bf16[4,4,2,64,1024]{4,3,2,1,0:T(8,128)(2,1)}, bf16[4,4,2,64,1024]{4,3,2,1,0:T(8,128)(2,1)}, bf16[4,4,2,64,1024]{4,3,2,1,0:T(8,128)(2,1)}, bf16[4,4...) custom-call(bf16[384,2048]{1,0:T(8,128)(2,1)} %bitcast.18, ...), custom_call_target="tpu_custom_call" | custom-call | tf_op jit(solution)/shard_map/forward/pallas_call | solution.py:786
  124.4 94.3 %backward.1 = (f32[384,2048]{1,0:T(8,128)}, bf16[4,192,1024]{2,1,0:T(8,128)(2,1)}, bf16[4,192,1024]{2,1,0:T(8,128)(2,1)}, f32[6,64,1024]{2,1,0:T(8,128)}, f32[8,2048]{1,0:T(8,128)}) custom-call(bf16[3,128,1024]{2,1,0:T(8,128)(2,1)} %get-tuple-element.40.od_any, bf16[3,128,1024]{2,1,0:T(8,128)(2,1)} %get-tuple-element.41.dkv_any, bf16[384,2048]{1,0:T(8,128)(2,1)} %bitcast.22, ...), custom_call_target="tpu_custom_call" | custom-call | tf_op jit(solution)/shard_map/backward/pallas_call | solution.py:1059
  218.7 6.4 %finish.1 = (f32[384,2048]{1,0:T(8,128)}, f32[384,2048]{1,0:T(8,128)}, f32[3,64,512]{2,1,0:T(8,128)}, f32[64,512]{1,0:T(8,128)}, f32[64,2048]{1,0:T(8,128)}, /*i...) custom-call(bf16[384,2048]{1,0:T(8,128)(2,1)} %bitcast.20, ...), custom_call_target="tpu_custom_call" | custom-call | tf_op jit(solution)/shard_map/finish/pallas_call | solution.py:1156
